TPU v7x, 32 devices: a whole 2x2x4 slice. The times are simulated.
32 devices in a mesh: clips: 2 (over y), tm: 4 (over z), space: 4 (over x, core).
Axes of the slice: x: 2, y: 2, z: 4, core: 2. Of those that a mesh axis runs over, the one named last changes fastest.
Arguments:
- latent: bfloat16 [16, 8, 16, 16], P(('clips', 'tm'), 'space'), parts along dimension 0, may hold values from -6 to 6
- w_in: bfloat16 [3, 3, 3, 16, 384], replicated, may hold values from -0.3125 to 0.3125
- b_in: float32 [384], replicated, may hold values from -1.5 to 1.5
- gain_in: float32 [384], replicated, may hold values from 0.1 to 1.9
- w_time: bfloat16 [3, 384, 768], replicated, may hold values from -0.1875 to 0.1875
- b_time: float32 [768], replicated, may hold values from -1.5 to 1.5
- w_up: bfloat16 [3, 3, 384, 192], replicated, may hold values from -0.109375 to 0.109375
- b_up: float32 [192], replicated, may hold values from -1.5 to 1.5
Outputs:
- decoded: bfloat16 [32, 16, 32, 192], P(('clips', 'tm'), 'space'), parts along dimension 0
There are 2 independent parts, one for each index of `clips`. A program takes and returns all parts, laid end to end along the dimension named above; an argument that names none is the same for every part. Nothing has to cross between parts.
All inputs are finite; a program needn't handle non-finite values.
Results may differ from a plain program's by a relative error of at most 0.0055.
Values may be sent and summed in bfloat16 or wider, within the bound.
No kernel may reach another device: no remote copies, remote signals or barrier semaphores. Data moves between devices by JAX's collectives and lax.ppermute only.
A program may use at most 64 MiB of HBM per device.

v0:
```python
import jax
import jax.numpy as jnp
from jax import lax
from jax.sharding import PartitionSpec as P

EPSILON = 1e-06


def with_halo(block, sides, width):
    for axis, dim in sides:
        count = lax.axis_size(axis)
        forward = [(i, i + 1) for i in range(count - 1)]
        backward = [(target, source) for source, target in forward]
        low = lax.ppermute(
            lax.slice_in_dim(block, block.shape[dim] - width, None, axis=dim), axis, forward
        )
        high = lax.ppermute(lax.slice_in_dim(block, 0, width, axis=dim), axis, backward)
        block = jnp.concatenate([low, block, high], axis=dim)
    return block


def passed_along(x, axis, by):
    count = lax.axis_size(axis)
    pairs = [(i, i + by) for i in range(count) if 0 <= i + by < count]
    return lax.ppermute(x, axis, pairs)


def margin_rows(joined):
    depth = 2
    return with_halo(joined, (("space", 1),), depth)


def entry_conv(extended, w_in, b_in, gain_in):
    frame_count = extended.shape[0] - 2
    row_count = extended.shape[1] - 2
    col_count = extended.shape[2]
    padded = jnp.pad(extended, ((0, 0), (0, 0), (1, 1), (0, 0)))
    tap_list = [
        padded[
            frame_tap : frame_tap + frame_count,
            row_tap : row_tap + row_count,
            col_tap : col_tap + col_count,
            :,
        ]
        for frame_tap in range(3)
        for row_tap in range(3)
        for col_tap in range(3)
    ]
    stacked = jnp.concatenate(tap_list, axis=3).reshape(frame_count * row_count * col_count, -1)
    hidden = (
        jnp.dot(stacked, w_in.reshape(stacked.shape[1], -1), preferred_element_type=jnp.float32)
        + b_in
    )
    inverse = lax.rsqrt(jnp.mean(hidden * hidden, axis=1, keepdims=True) + EPSILON)
    normed = jax.nn.silu(hidden * inverse * gain_in).astype(jnp.bfloat16)
    return normed.reshape(frame_count, row_count, col_count, -1)


def time_conv(extended, w_time, b_time):
    frame_count = extended.shape[0] - 2
    row_count = extended.shape[1]
    col_count = extended.shape[2]
    feature_width = extended.shape[3]
    tap_list = [extended[offset : offset + frame_count] for offset in range(3)]
    stacked = jnp.concatenate(tap_list, axis=3).reshape(
        frame_count * row_count * col_count, 3 * feature_width
    )
    result = (
        jnp.dot(stacked, w_time.reshape(3 * feature_width, -1), preferred_element_type=jnp.float32)
        + b_time
    )
    return result.astype(jnp.bfloat16).reshape(frame_count, row_count, col_count, -1)


def clear_outside(timed):
    row_total = timed.shape[1]
    position = lax.axis_index("space")
    space_count = lax.axis_size("space")
    row_ids = jnp.arange(row_total, dtype=jnp.int32)
    row_valid = ((row_ids > 0) | (position > 0)) & (
        (row_ids < row_total - 1) | (position < space_count - 1)
    )
    return jnp.where(row_valid[None, :, None, None], timed, jnp.zeros_like(timed))


def upsample_conv(timed, w_up, b_up):
    frame_count, row_total, col_count, double_width = timed.shape
    feature_width = double_width // 2
    halves = timed.reshape(frame_count, row_total, col_count, 2, feature_width)
    doubled = jnp.moveaxis(halves, 3, 1).reshape(
        2 * frame_count, row_total, col_count, feature_width
    )
    enlarged = jnp.repeat(jnp.repeat(doubled, 2, axis=1), 2, axis=2)[:, 1 : 2 * row_total - 1]
    padded = jnp.pad(enlarged, ((0, 0), (0, 0), (1, 1), (0, 0)))
    out_rows = 2 * row_total - 4
    out_cols = 2 * col_count
    tap_list = [
        padded[:, row_tap : row_tap + out_rows, col_tap : col_tap + out_cols, :]
        for row_tap in range(3)
        for col_tap in range(3)
    ]
    stacked = jnp.concatenate(tap_list, axis=3).reshape(
        2 * frame_count * out_rows * out_cols, 9 * feature_width
    )
    result = (
        jnp.dot(stacked, w_up.reshape(9 * feature_width, -1), preferred_element_type=jnp.float32)
        + b_up
    )
    return result.astype(jnp.bfloat16).reshape(2 * frame_count, out_rows, out_cols, -1)


def shards(latent, w_in, b_in, gain_in, w_time, b_time, w_up, b_up):
    earlier = passed_along(latent, "tm", 1)
    joined = jnp.concatenate([earlier, latent], axis=0)
    active = entry_conv(margin_rows(joined), w_in, b_in, gain_in)
    previous = passed_along(active, "tm", 1)
    context = jnp.concatenate([previous, active], axis=0)
    timed = clear_outside(time_conv(context, w_time, b_time))
    return upsample_conv(timed, w_up, b_up)


def solution(mesh):
    in_specs = (P(("clips", "tm"), "space", None, None), P(), P(), P(), P(), P(), P(), P())
    out_specs = P(("clips", "tm"), "space", None, None)
    return jax.shard_map(shards, mesh=mesh, in_specs=in_specs, out_specs=out_specs, check_vma=False)
```

profile of v0, /device:TPU:18, one launch (start us, length us, event | category | flops | bytes accessed | tf_op | source)
XLA Modules:
  0.0 33.7 jit_solution(15161917546235122889)
XLA Ops:
  0.0 3.6 %collective-permute-start = (bf16[2,2,16,16]{3,2,1,0:T(8,128)(2,1)}, bf16[2,2,16,16]{3,2,1,0:T(8,128)(2,1)S(1)}, u32[]{:S(2)}, u32[]{:S(2)}) collective-permute-start(bf16[2,2,16,16]{3,2,1,0:T(8,128)(2,1)} %param.8), channel_id=1, source_target_pairs={{0,4},{4,8},{8,12},{1,5},{5,9},{9,13},{2,6},{6,10},{10,14},{3,7},{... | collective-permute-start | bytes 6152 | tf_op jit(solution)/shard_map/ppermute | solution.py:25
  3.6 2.4 %collective-permute-done = bf16[2,2,16,16]{3,2,1,0:T(8,128)(2,1)S(1)} collective-permute-done((bf16[2,2,16,16]{3,2,1,0:T(8,128)(2,1)}, bf16[2,2,16,16]{3,2,1,0:T(8,128)(2,1)S(1)}, u32[]{:S(2)}, u32[]{:S(2)}) %collective-permute-start) | collective-permute-done | bytes 2080 | tf_op jit(solution)/shard_map/ppermute | solution.py:25
  6.0 0.6 %constant_dynamic-update-slice_fusion.1 = bf16[4,2,16,16]{3,2,1,0:T(8,128)(2,1)} fusion(bf16[2,2,16,16]{3,2,1,0:T(8,128)(2,1)S(1)} %collective-permute-done), kind=kLoop, calls=%fused_computation.64 | loop fusion | bytes 18432
  6.6 1.3 %constant_dynamic-update-slice_fusion = bf16[4,2,16,16]{3,2,1,0:T(8,128)(2,1)} fusion(bf16[4,2,16,16]{3,2,1,0:T(8,128)(2,1)} %constant_dynamic-update-slice_fusion.1, bf16[2,2,16,16]{3,2,1,0:T(8,128)(2,1)} %param.8), kind=kLoop, calls=%fused_computation.63 | loop fusion | bytes 32768 | tf_op jit(solution)/shard_map/concatenate | solution.py:114
  7.9 1.9 %collective-permute-start.1 = (bf16[4,2,16,16]{3,2,1,0:T(8,128)(2,1)}, bf16[4,2,16,16]{3,2,1,0:T(8,128)(2,1)}, u32[]{:S(2)}, u32[]{:S(2)}) collective-permute-start(bf16[4,2,16,16]{3,2,1,0:T(8,128)(2,1)} %constant_dynamic-update-slice_fusion), channel_id=1, source_target_pairs={{0,1},{1,2},{2,3},{4,5},{5,6},{6,7},{8,9},{9,10},{10,11},{12,13},{... | collective-permute-start | bytes 12296 | tf_op jit(solution)/shard_map/ppermute | solution.py:14
  9.8 3.6 %collective-permute-start.2 = (bf16[4,2,16,16]{3,2,1,0:T(8,128)(2,1)}, bf16[4,2,16,16]{3,2,1,0:T(8,128)(2,1)}, u32[]{:S(2)}, u32[]{:S(2)}) collective-permute-start(bf16[4,2,16,16]{3,2,1,0:T(8,128)(2,1)} %constant_dynamic-update-slice_fusion), channel_id=1, source_target_pairs={{1,0},{2,1},{3,2},{5,4},{6,5},{7,6},{9,8},{10,9},{11,10},{13,12},{... | collective-permute-start | bytes 12296 | tf_op jit(solution)/shard_map/ppermute | solution.py:17
  13.5 2.5 %copy.10 = bf16[3,3,384,192]{2,1,0,3:T(4,128)(2,1)S(1)} copy(bf16[3,3,384,192]{2,3,1,0:T(8,128)(2,1)} %param.14) | data formatting | bytes 2654208 | tf_op args[6]
  16.0 2.4 %reshape.69 = bf16[3456,192]{0,1:T(8,128)(2,1)} reshape(bf16[3,3,384,192]{2,1,0,3:T(4,128)(2,1)S(1)} %copy.10) | data formatting | bytes 2654208 | tf_op jit(solution)/shard_map/reshape | solution.py:106
  18.3 0.8 %pad_maximum_fusion.2 = bf16[4,6,16,16]{3,2,1,0:T(8,128)(2,1)S(1)} fusion(bf16[4,2,16,16]{3,2,1,0:T(8,128)(2,1)} %collective-permute-done.2, bf16[4,2,16,16]{3,2,1,0:T(8,128)(2,1)} %constant_dynamic-update-slice_fusion, bf16[4,2,16,16]{3,2,1,0:T(8,128)(2,1)} %collective-permute-done.1), kind=kLoop, calls=%fused_computation.48 | loop fusion | flops 12288 | bytes 24576 | tf_op jit(solution)/shard_map/concatenate | solution.py:18
  19.2 0.1 pad_slice_fusion.6
  19.3 1.0 %pad_maximum_fusion.3 = (bf16[2,4,16,16]{3,2,1,0:T(8,128)(2,1)S(1)}, bf16[2,4,16,16]{3,2,1,0:T(8,128)(2,1)S(1)}, bf16[2,4,16,16]{3,2,1,0:T(8,128)(2,1)S(1)}, bf1...) fusion(bf16[4,2,16,16]{3,2,1,0:T(8,128)(2,1)} %collective-permu, ...), kind=kLoop, calls=%fused_computation.61 | loop fusion | flops 49152 | bytes 176128 | tf_op jit(solution)/shard_map/concatenate | solution.py:18
  20.3 0.3 %concatenate.40 = bf16[2,4,16,432]{3,2,1,0:T(8,128)(2,1)S(1)} concatenate(bf16[2,4,16,16]{3,2,1,0:T(8,128)(2,1)S(1)} %get-tuple-element.39, bf16[2,4,16,16]{3,2,1,0:T(8,128)(2,1)S(1)} %get-tuple-element.35, bf16[2,4,16,16]{3,2,1,0:T(8,128)(2,1)S(1)} %get-tuple-element.8, bf16[2,4,16,16]{3,2,1,0:T(8,128)(2,1)S(1)} %get-tuple-element.9, ...), dimensions={3} | concatenate | bytes 221184 | tf_op jit(solution)/shard_map/concatenate | solution.py:49
  20.6 1.3 %multiply_reduce_fusion = (f32[128]{0:T(128)S(1)}, f32[128,384]{1,0:T(8,128)S(1)}) fusion(f32[384]{0:T(512)S(1)} %copy-done.2, bf16[128,432]{1,0:T(8,128)(2,1)S(1)} %bitcast.21, bf16[432,384]{1,0:T(8,128)(2,1)} %bitcast.24), kind=kOutput, calls=%fused_computation.45 | convolution fusion | flops 42614656 | bytes 641024 | tf_op jit(solution)/shard_map/dot_general | solution.py:51
  21.9 0.1 multiply_convert_fusion
  22.1 3.5 %collective-permute-start.3 = (bf16[2,4,16,384]{3,2,1,0:T(8,128)(2,1)S(1)}, bf16[2,4,16,384]{3,2,1,0:T(8,128)(2,1)S(1)}, u32[]{:S(2)}, u32[]{:S(2)}) collective-permute-start(bf16[2,4,16,384]{3,2,1,0:T(8,128)(2,1)S(1)} %bitcast.22), channel_id=1, source_target_pairs={{0,4},{4,8},{8,12},{1,5},{5,9},{9,13},{2,6},{6,10},{10,14},{3,7},{... | collective-permute-start | bytes 294920 | tf_op jit(solution)/shard_map/ppermute | solution.py:25
  25.6 3.0 %collective-permute-done.3 = bf16[2,4,16,384]{3,2,1,0:T(8,128)(2,1)S(1)} collective-permute-done((bf16[2,4,16,384]{3,2,1,0:T(8,128)(2,1)S(1)}, bf16[2,4,16,384]{3,2,1,0:T(8,128)(2,1)S(1)}, u32[]{:S(2)}, u32[]{:S(2)}) %collective-permute-start.3) | collective-permute-done | bytes 98336 | tf_op jit(solution)/shard_map/ppermute | solution.py:25
  28.6 0.4 %fusion = bf16[128,768]{1,0:T(8,128)(2,1)S(1)} fusion(bf16[1152,768]{1,0:T(8,128)(2,1)S(1)} %bitcast.18, bf16[128,384]{1,0:T(8,128)(2,1)S(1)} %multiply_convert_fusion, bf16[128,384]{1,0:T(8,128)(2,1)S(1)} %bitcast.27, bf16[128,384]{1,0:T(8,128)(2,1)S(1)} %bitcast.26, f32[768]{0:T(1024)S(1)} %copy-done.4), kind=kOutput, calls=%fused_computation.2 | convolution fusion | flops 227573760 | bytes 2264064 | tf_op jit(solution)/shard_map/dot_general | solution.py:69
  29.1 0.1 broadcast_select_fusion
  29.3 0.5 %broadcast_in_dim.26 = bf16[4,8,16,2,384]{4,3,2,1,0:T(2,128)(2,1)S(1)} broadcast(bf16[4,8,16,384]{3,2,1,0:T(8,128)(2,1)S(1)} %bitcast.19), dimensions={0,1,2,4} | broadcast | bytes 1179648 | tf_op jit(solution)/shard_map/broadcast_in_dim | solution.py:93
  29.7 0.3 reshape.67
  30.0 0.1 slice.194
  30.1 0.1 fusion.2
  30.2 0.1 slice_dynamic-update-slice_fusion.2
  30.3 0.1 fusion.3
  30.4 0.1 fusion.4
  30.6 0.1 slice_dynamic-update-slice_fusion.1
  30.7 0.1 fusion.5
  30.8 0.1 fusion.6
  31.0 0.1 fusion.7
  31.2 0.4 %copy-done.1 = bf16[3456,192]{0,1:T(8,128)(2,1)S(1)} copy-done((bf16[3456,192]{0,1:T(8,128)(2,1)S(1)}, bf16[3456,192]{0,1:T(8,128)(2,1)}, u32[]{:S(2)}) %copy-start.1) | copy-done | bytes 1327128
  31.5 1.3 %fusion.1 = bf16[512,192]{0,1:T(8,128)(2,1)S(1)} fusion(bf16[512,3456]{1,0:T(8,128)(2,1)S(1)} %bitcast.28, bf16[3456,192]{0,1:T(8,128)(2,1)S(1)} %copy-done.1, f32[192]{0:T(256)S(1)} %copy-done.5), kind=kOutput, calls=%fused_computation.3 | convolution fusion | flops 679673856 | bytes 5063424 | tf_op jit(solution)/shard_map/dot_general | solution.py:106
  32.8 0.8 %copy.11 = bf16[512,192]{1,0:T(8,128)(2,1)} copy(bf16[512,192]{0,1:T(8,128)(2,1)S(1)} %fusion.1) | data formatting | bytes 393216 | tf_op jit(solution)/shard_map/convert_element_type | solution.py:109
  (20 shorter events, 0.2 us)
Async XLA Ops:
  0.0 28.6 %copy-start = (bf16[3,384,768]{2,1,0:T(8,128)(2,1)S(1)}, bf16[3,384,768]{2,1,0:T(8,128)(2,1)}, u32[]{:S(2)}) copy-start(bf16[3,384,768]{2,1,0:T(8,128)(2,1)} %param.12) | copy-start | bytes 5308420
  0.0 6.0 %collective-permute-start = (bf16[2,2,16,16]{3,2,1,0:T(8,128)(2,1)}, bf16[2,2,16,16]{3,2,1,0:T(8,128)(2,1)S(1)}, u32[]{:S(2)}, u32[]{:S(2)}) collective-permute-start(bf16[2,2,16,16]{3,2,1,0:T(8,128)(2,1)} %param.8), channel_id=1, source_target_pairs={{0,4},{4,8},{8,12},{1,5},{5,9},{9,13},{2,6},{6,10},{10,14},{3,7},{... | collective-permute-start | bytes 6152 | tf_op jit(solution)/shard_map/ppermute | solution.py:25
  7.9 10.4 %collective-permute-start.1 = (bf16[4,2,16,16]{3,2,1,0:T(8,128)(2,1)}, bf16[4,2,16,16]{3,2,1,0:T(8,128)(2,1)}, u32[]{:S(2)}, u32[]{:S(2)}) collective-permute-start(bf16[4,2,16,16]{3,2,1,0:T(8,128)(2,1)} %constant_dynamic-update-slice_fusion), channel_id=1, source_target_pairs={{0,1},{1,2},{2,3},{4,5},{5,6},{6,7},{8,9},{9,10},{10,11},{12,13},{... | collective-permute-start | bytes 12296 | tf_op jit(solution)/shard_map/ppermute | solution.py:14
  9.8 8.5 %collective-permute-start.2 = (bf16[4,2,16,16]{3,2,1,0:T(8,128)(2,1)}, bf16[4,2,16,16]{3,2,1,0:T(8,128)(2,1)}, u32[]{:S(2)}, u32[]{:S(2)}) collective-permute-start(bf16[4,2,16,16]{3,2,1,0:T(8,128)(2,1)} %constant_dynamic-update-slice_fusion), channel_id=1, source_target_pairs={{1,0},{2,1},{3,2},{5,4},{6,5},{7,6},{9,8},{10,9},{11,10},{13,12},{... | collective-permute-start | bytes 12296 | tf_op jit(solution)/shard_map/ppermute | solution.py:17
  15.9 4.7 %copy-start.2 = (f32[384]{0:T(512)S(1)}, f32[384]{0:T(512)}, u32[]{:S(2)}) copy-start(f32[384]{0:T(512)} %param.10) | copy-start | bytes 4612
  16.0 6.0 %copy-start.3 = (f32[384]{0:T(512)S(1)}, f32[384]{0:T(512)}, u32[]{:S(2)}) copy-start(f32[384]{0:T(512)} %param.11) | copy-start | bytes 4612
  16.0 12.6 %copy-start.4 = (f32[768]{0:T(1024)S(1)}, f32[768]{0:T(1024)}, u32[]{:S(2)}) copy-start(f32[768]{0:T(1024)} %param.13) | copy-start | bytes 9220
  22.1 6.5 %collective-permute-start.3 = (bf16[2,4,16,384]{3,2,1,0:T(8,128)(2,1)S(1)}, bf16[2,4,16,384]{3,2,1,0:T(8,128)(2,1)S(1)}, u32[]{:S(2)}, u32[]{:S(2)}) collective-permute-start(bf16[2,4,16,384]{3,2,1,0:T(8,128)(2,1)S(1)} %bitcast.22), channel_id=1, source_target_pairs={{0,4},{4,8},{8,12},{1,5},{5,9},{9,13},{2,6},{6,10},{10,14},{3,7},{... | collective-permute-start | bytes 294920 | tf_op jit(solution)/shard_map/ppermute | solution.py:25
  30.2 1.3 %copy-start.1 = (bf16[3456,192]{0,1:T(8,128)(2,1)S(1)}, bf16[3456,192]{0,1:T(8,128)(2,1)}, u32[]{:S(2)}) copy-start(bf16[3456,192]{0,1:T(8,128)(2,1)} %reshape.69) | copy-start | bytes 3981316
  30.2 1.3 %copy-start.5 = (f32[192]{0:T(256)S(1)}, f32[192]{0:T(256)}, u32[]{:S(2)}) copy-start(f32[192]{0:T(256)} %param.15) | copy-start | bytes 2308
where the time goes:
time: 34.2 us; the launch traced here: 33.7 us
  starting transfers between devices  12.6 us (37%)
  local copies, waits for them, and re-layouts  10.3 us (30%)
  waiting for transfers between devices  5.36 us (16%)
  matrix products  3.02 us (9%)
  other arithmetic  2.06 us (6%)
    ppermute x2, starting transfers between devices, passed_along(): return lax.ppermute(x, axis, pairs)  7.09 us
    ppermute x2, waiting for transfers between devices, passed_along(): return lax.ppermute(x, axis, pairs)  5.35 us
    unnamed x22, local copies, waits for them, and re-layouts  4.32 us
    ppermute x1, starting transfers between devices, with_halo(): lax.ppermute(lax.slice_in_dim(block, 0, width, axis=dim), axis, backward)  3.64 us
    reshape x1, local copies, waits for them, and re-layouts, upsample_conv(): w_up.reshape(9 * feature_width, -1)  2.36 us
    ppermute x1, starting transfers between devices, with_halo(): lax.ppermute(lax.slice_in_dim(block, block.shape[dim] - width, None, axis...  1.91 us
    concatenate x2, other arithmetic, with_halo(): block = jnp.concatenate([low, block, high], axis=dim)  1.78 us
    concatenate x1, local copies, waits for them, and re-layouts, shards(): joined = jnp.concatenate([earlier, latent], axis=0)  1.32 us
  transfers between devices with their start and end apart: 4, of which 2 were waited for; matrix products, arithmetic and copies ran while one was open for 14% of the time, Pallas kernels for 0%

commit v1 on v0

v1 whole, which is shorter than its diff:
```python
import functools

import jax
import jax.numpy as jnp
from jax import lax
from jax.experimental import pallas as pl
from jax.experimental.pallas import tpu as pltpu
from jax.sharding import PartitionSpec as P

EPSILON = 1e-06
LANES = 128


def swapped(x, axis, first):
    count = lax.axis_size(axis)
    pairs = []
    for low in range(first, first + count, 2):
        a, b = low % count, (low + 1) % count
        pairs += [(a, b), (b, a)]
    return lax.ppermute(x, axis, pairs)


def shifted(x, axis, by):
    count = lax.axis_size(axis)
    return lax.ppermute(x, axis, [(i, (i + by) % count) for i in range(count)])


def pack_kernel(own_ref, even_ref, odd_ref, packed_ref):
    space, count = lax.axis_index("space"), lax.axis_size("space")
    frames, rows, cols, width = own_ref.shape
    is_even = lax.rem(space, 2) == 0
    even, odd = even_ref[...], odd_ref[...]
    above = jnp.where(space > 0, jnp.where(is_even, odd, even), jnp.zeros_like(even))
    below = jnp.where(space < count - 1, jnp.where(is_even, even, odd), jnp.zeros_like(even))
    channel = lax.broadcasted_iota(jnp.int32, (width, LANES), 0)
    lane = lax.broadcasted_iota(jnp.int32, (width, LANES), 1)
    total = jnp.zeros((frames * cols, LANES), jnp.float32)
    for r, block in enumerate([x[:, r] for x in (above, own_ref[...], below) for r in range(rows)]):
        spread = (lane == channel + r * width).astype(own_ref.dtype)
        total += jnp.dot(block.reshape(frames * cols, width), spread, preferred_element_type=jnp.float32)
    packed_ref[...] = total.astype(own_ref.dtype).reshape(packed_ref.shape)


def stage_kernel(*refs):
    count = (len(refs) - 1) // 2
    copies = [pltpu.make_async_copy(refs[i], refs[count + i], refs[-1].at[i]) for i in range(count)]
    for copy in copies:
        copy.start()
    for copy in copies:
        copy.wait()


def column_shift(x, by, cols):
    column = lax.rem(lax.broadcasted_iota(jnp.int32, x.shape, 0), cols)
    edge = 0 if by > 0 else cols - 1
    return jnp.where(column == edge, 0.0, pltpu.roll(x, by % x.shape[0], axis=0))


def main_kernel(
    own_ref, one_ref, two_ref, w_in_ref, b_in_ref, gain_ref, w_time_ref, b_time_ref, w_up_ref, b_up_ref, out_ref,
    *, rows, width,
):
    time, space, space_count = lax.axis_index("tm"), lax.axis_index("space"), lax.axis_size("space")
    own_frames, cols, _ = own_ref.shape
    tall = rows + 2
    features = w_in_ref.shape[1]
    one = jnp.where(time > 0, one_ref[...], jnp.zeros_like(one_ref))
    two = jnp.where(time > 1, two_ref[...], jnp.zeros_like(two_ref))
    frames = jnp.concatenate([two, one, own_ref[...]], axis=0).astype(jnp.float32)
    frame_total = frames.shape[0]
    flat = frames.reshape(frame_total * cols, LANES)
    taps = []
    for shift in (1, 0, -1):
        moved = column_shift(flat, shift, cols) if shift else flat
        rolled = [moved if r == 0 else pltpu.roll(moved, LANES - r * width, axis=1) for r in range(tall)]
        stacked = jnp.stack([x.astype(jnp.bfloat16).reshape(frame_total, cols, LANES) for x in rolled], axis=1)
        taps.append(stacked.reshape(frame_total * tall * cols, LANES))
    block = tall * cols
    active_frames = frame_total - 2
    left, right = [], []
    blank = jnp.zeros((LANES - 3 * width, features), jnp.bfloat16)
    for a in range(3):
        for e in range(3):
            left.append(taps[e][a * block : (a + active_frames) * block])
            for b in range(3):
                start = ((a * 3 + b) * 3 + e) * width
                right.append(w_in_ref[start : start + width, :])
            right.append(blank)
    hidden = jnp.dot(
        jnp.concatenate(left, axis=1), jnp.concatenate(right, axis=0), preferred_element_type=jnp.float32
    )
    hidden = hidden + b_in_ref[...][None, :]
    inverse = lax.rsqrt(jnp.mean(hidden * hidden, axis=1, keepdims=True) + EPSILON)
    v = hidden * inverse * gain_ref[...][None, :]
    half = 0.5 * v
    active = half + half * jnp.tanh(half)
    frame_id = lax.broadcasted_iota(jnp.int32, active.shape, 0) // block
    active = jnp.where((frame_id >= active_frames - own_frames) | (time > 0), active, 0.0).astype(jnp.bfloat16)

    stacked = jnp.concatenate([active[a * block : (a + own_frames) * block] for a in range(3)], axis=1)
    timed = jnp.dot(stacked, w_time_ref[...], preferred_element_type=jnp.float32) + b_time_ref[...][None, :]
    row = lax.rem(lax.broadcasted_iota(jnp.int32, timed.shape, 0) // cols, tall)
    inside = ((row > 0) | (space > 0)) & ((row < tall - 1) | (space < space_count - 1))
    timed = jnp.where(inside, timed, 0.0).astype(jnp.bfloat16)

    out_rows = 2 * rows
    out_width = w_up_ref.shape[0] // 9
    left = []
    for b in range(3):
        picks = []
        for f in range(own_frames):
            for h in range(2):
                for i in range(out_rows):
                    r = (i + b - 1) // 2 + 1
                    picks.append(timed[(f * tall + r) * cols : (f * tall + r + 1) * cols, h * features : (h + 1) * features])
        left.append(jnp.concatenate(picks, axis=0))
    sums = []
    for e in range(3):
        total = None
        for b in range(3):
            tap = w_up_ref[(b * 3 + e) * out_width : (b * 3 + e + 1) * out_width, :]
            part = lax.dot_general(left[b], tap, (((1,), (1,)), ((), ())), preferred_element_type=jnp.float32)
            total = part if total is None else total + part
        sums.append(total)
    middle = sums[1] + b_up_ref[...][None, :]
    even = column_shift(sums[0], 1, cols) + (middle + sums[2])
    odd = column_shift(sums[2], -1, cols) + (middle + sums[0])
    both = jnp.stack([even, odd], axis=1).reshape(2 * even.shape[0], out_width)
    out_ref[...] = both.astype(jnp.bfloat16).reshape(out_ref.shape)


def shards(latent, w_in, b_in, gain_in, w_time, b_time, w_up, b_up):
    own_frames, rows, cols, width = latent.shape
    features = w_in.shape[-1]
    out_width = w_up.shape[-1]
    vmem = pl.BlockSpec(memory_space=pltpu.VMEM)
    even = swapped(latent, "space", 0)
    odd = swapped(latent, "space", 1)
    own = pl.pallas_call(
        pack_kernel,
        out_shape=jax.ShapeDtypeStruct((own_frames, cols, LANES), latent.dtype),
        in_specs=[vmem] * 3,
        out_specs=vmem,
        compiler_params=pltpu.CompilerParams(vmem_limit_bytes=1024 * 1024),
    )(latent, even, odd)
    two = shifted(own, "tm", 2)
    one = shifted(own, "tm", 1)
    weights = (
        w_in.reshape(-1, features), b_in, gain_in, w_time.reshape(-1, w_time.shape[-1]), b_time,
        jnp.swapaxes(w_up, 2, 3).reshape(-1, w_up.shape[2]), b_up,
    )
    staged = pl.pallas_call(
        stage_kernel,
        out_shape=[pltpu.VMEM(w.shape, w.dtype) for w in weights],
        in_specs=[pl.BlockSpec(memory_space=pltpu.HBM)] * len(weights),
        out_specs=[vmem] * len(weights),
        scratch_shapes=[pltpu.SemaphoreType.DMA((len(weights),))],
        compiler_params=pltpu.CompilerParams(vmem_limit_bytes=1024 * 1024),
    )(*[pltpu.with_memory_space_constraint(w, pltpu.HBM) for w in weights])
    return pl.pallas_call(
        functools.partial(main_kernel, rows=rows, width=width),
        out_shape=jax.ShapeDtypeStruct((2 * own_frames, 2 * rows, 2 * cols, out_width), jnp.bfloat16),
        in_specs=[vmem] * 10,
        out_specs=vmem,
        compiler_params=pltpu.CompilerParams(vmem_limit_bytes=16 * 1024 * 1024),
    )(own, one, two, *staged)


def solution(mesh):
    in_specs = (P(("clips", "tm"), "space", None, None), P(), P(), P(), P(), P(), P(), P())
    out_specs = P(("clips", "tm"), "space", None, None)
    return jax.shard_map(shards, mesh=mesh, in_specs=in_specs, out_specs=out_specs, check_vma=False)
```

time: 34.2 us -> 17.2 us (0.50)
  the two profiles are of different devices: /device:TPU:18 before, /device:TPU:0 now
where the time goes in v1:
time: 17.2 us; the launch traced here: 17 us
  starting transfers between devices  7.36 us (43%)
  Pallas kernels  5.48 us (32%)
  waiting for transfers between devices  3.43 us (20%)
  local copies, waits for them, and re-layouts  0.72 us (4%)
    ppermute x2, starting transfers between devices, shifted(): return lax.ppermute(x, axis, [(i, (i + by) % count) for i in range(count)])  4.3 us
    pallas_call x1, Pallas kernels, shards(): pl.pallas_call(functools.partial(main_kernel, rows=rows, width=width), ou...  3.28 us
    ppermute x2, starting transfers between devices, swapped(): return lax.ppermute(x, axis, pairs)  3.05 us
    pallas_call x1, Pallas kernels, shards(): pl.pallas_call(stage_kernel, out_shape=[pltpu.VMEM(w.shape, w.dtype) for...  2.08 us
    ppermute x2, waiting for transfers between devices, shifted(): return lax.ppermute(x, axis, [(i, (i + by) % count) for i in range(count)])  1.78 us
    ppermute x2, waiting for transfers between devices, swapped(): return lax.ppermute(x, axis, pairs)  1.65 us
    unnamed x2, local copies, waits for them, and re-layouts  0.72 us
  transfers between devices with their start and end apart: 4, of which 2 were waited for; matrix products, arithmetic and copies ran while one was open for 0% of the time, Pallas kernels for 12%

profile of v1, /device:TPU:0, one launch (start us, length us, event | category | flops | bytes accessed | tf_op | source)
XLA Modules:
  0.0 17.0 jit_solution(13501671675777641679)
XLA Ops:
  0.0 0.5 %collective-permute-start = (bf16[2,2,16,16]{3,2,1,0:T(8,128)(2,1)}, bf16[2,2,16,16]{3,2,1,0:T(8,128)(2,1)S(1)}, u32[]{:S(2)}, u32[]{:S(2)}) collective-permute-start(bf16[2,2,16,16]{3,2,1,0:T(8,128)(2,1)} %own_ref.1), channel_id=1, source_target_pairs={{0,1},{1,0},{2,3},{3,2},{4,5},{5,4},{6,7},{7,6},{8,9},{9,8},{10,11... | collective-permute-start | bytes 6152 | tf_op jit(solution)/shard_map/ppermute | solution.py:20
  0.5 2.6 %collective-permute-start.1 = (bf16[2,2,16,16]{3,2,1,0:T(8,128)(2,1)}, bf16[2,2,16,16]{3,2,1,0:T(8,128)(2,1)S(1)}, u32[]{:S(2)}, u32[]{:S(2)}) collective-permute-start(bf16[2,2,16,16]{3,2,1,0:T(8,128)(2,1)} %own_ref.1), channel_id=1, source_target_pairs={{1,2},{2,1},{3,0},{0,3},{5,6},{6,5},{7,4},{4,7},{9,10},{10,9},{11,... | collective-permute-start | bytes 6152 | tf_op jit(solution)/shard_map/ppermute | solution.py:20
  3.1 0.0 collective-permute-done.even_ref
  3.1 1.7 %collective-permute-done.1.odd_ref = bf16[2,2,16,16]{3,2,1,0:T(8,128)(2,1)S(1)} collective-permute-done((bf16[2,2,16,16]{3,2,1,0:T(8,128)(2,1)}, bf16[2,2,16,16]{3,2,1,0:T(8,128)(2,1)S(1)}, u32[]{:S(2)}, u32[]{:S(2)}) %collective-permute-start.1) | collective-permute-done | bytes 2080 | tf_op jit(solution)/shard_map/ppermute | solution.py:20
  4.7 0.0 copy-start
  4.7 0.7 %copy-done = bf16[2,2,16,16]{3,2,1,0:T(8,128)(2,1)S(1)} copy-done((bf16[2,2,16,16]{3,2,1,0:T(8,128)(2,1)S(1)}, bf16[2,2,16,16]{3,2,1,0:T(8,128)(2,1)}, u32[]{:S(2)}) %copy-start) | copy-done | bytes 2072
  5.4 0.1 shard_map.82.own_ref
  5.6 2.7 %collective-permute-start.3 = (bf16[2,16,128]{2,1,0:T(8,128)(2,1)S(1)}, bf16[2,16,128]{2,1,0:T(8,128)(2,1)S(1)}, u32[]{:S(2)}, u32[]{:S(2)}) collective-permute-start(bf16[2,16,128]{2,1,0:T(8,128)(2,1)S(1)} %shard_map.82.own_ref), channel_id=1, source_target_pairs={{0,8},{4,12},{8,0},{12,4},{1,9},{5,13},{9,1},{13,5},{2,10},{6,14},... | collective-permute-start | bytes 24584 | tf_op jit(solution)/shard_map/ppermute | solution.py:25
  8.3 1.6 %collective-permute-start.2 = (bf16[2,16,128]{2,1,0:T(8,128)(2,1)S(1)}, bf16[2,16,128]{2,1,0:T(8,128)(2,1)S(1)}, u32[]{:S(2)}, u32[]{:S(2)}) collective-permute-start(bf16[2,16,128]{2,1,0:T(8,128)(2,1)S(1)} %shard_map.82.own_ref), channel_id=1, source_target_pairs={{0,4},{4,8},{8,12},{12,0},{1,5},{5,9},{9,13},{13,1},{2,6},{6,10},{... | collective-permute-start | bytes 24584 | tf_op jit(solution)/shard_map/ppermute | solution.py:25
  9.9 2.1 %shard_map.83 = (bf16[432,384]{1,0:T(8,128)(2,1)S(1)}, f32[384]{0:T(512)S(1)}, f32[384]{0:T(512)S(1)}, bf16[1152,768]{1,0:T(8,128)(2,1)S(1)}, f32[768]{0:T(1024)...) custom-call(bf16[432,384]{1,0:T(8,128)(2,1)} %bitcast.7, f32[384]{0:T(512)} %refs_1_.1, f32[384]{0:T(512)} %refs_2_.1, ...), custom_call_target="tpu_custom_call" | custom-call | tf_op jit(solution)/shard_map/pallas_call | solution.py:152
  11.9 0.0 collective-permute-done.3.two_ref
  12.0 1.8 %collective-permute-done.2.one_ref = bf16[2,16,128]{2,1,0:T(8,128)(2,1)S(1)} collective-permute-done((bf16[2,16,128]{2,1,0:T(8,128)(2,1)S(1)}, bf16[2,16,128]{2,1,0:T(8,128)(2,1)S(1)}, u32[]{:S(2)}, u32[]{:S(2)}) %collective-permute-start.2) | collective-permute-done | bytes 8224 | tf_op jit(solution)/shard_map/ppermute | solution.py:25
  13.7 3.3 %shard_map.84 = bf16[4,4,32,192]{3,2,1,0:T(8,128)(2,1)} custom-call(bf16[2,16,128]{2,1,0:T(8,128)(2,1)S(1)} %shard_map.82.own_ref, bf16[2,16,128]{2,1,0:T(8,128)(2,1)S(1)} %collective-permute-done.2.one_ref, bf16[2,16,128]{2,1,0:T(8,128)(2,1)S(1)} %collective-permute-done.3.two_ref, bf16[432,384]{1,0:T(8,128)(2,1)S(1)} %get-tuple-element.12.w_in_ref, ...), custom_call_target="tpu_custom_call" | custom-call | tf_op jit(solution)/shard_map/pallas_call | solution.py:160
Async XLA Ops:
  0.0 3.1 %collective-permute-start = (bf16[2,2,16,16]{3,2,1,0:T(8,128)(2,1)}, bf16[2,2,16,16]{3,2,1,0:T(8,128)(2,1)S(1)}, u32[]{:S(2)}, u32[]{:S(2)}) collective-permute-start(bf16[2,2,16,16]{3,2,1,0:T(8,128)(2,1)} %own_ref.1), channel_id=1, source_target_pairs={{0,1},{1,0},{2,3},{3,2},{4,5},{5,4},{6,7},{7,6},{8,9},{9,8},{10,11... | collective-permute-start | bytes 6152 | tf_op jit(solution)/shard_map/ppermute | solution.py:20
  0.5 4.3 %collective-permute-start.1 = (bf16[2,2,16,16]{3,2,1,0:T(8,128)(2,1)}, bf16[2,2,16,16]{3,2,1,0:T(8,128)(2,1)S(1)}, u32[]{:S(2)}, u32[]{:S(2)}) collective-permute-start(bf16[2,2,16,16]{3,2,1,0:T(8,128)(2,1)} %own_ref.1), channel_id=1, source_target_pairs={{1,2},{2,1},{3,0},{0,3},{5,6},{6,5},{7,4},{4,7},{9,10},{10,9},{11,... | collective-permute-start | bytes 6152 | tf_op jit(solution)/shard_map/ppermute | solution.py:20
  4.7 0.7 %copy-start = (bf16[2,2,16,16]{3,2,1,0:T(8,128)(2,1)S(1)}, bf16[2,2,16,16]{3,2,1,0:T(8,128)(2,1)}, u32[]{:S(2)}) copy-start(bf16[2,2,16,16]{3,2,1,0:T(8,128)(2,1)} %own_ref.1) | copy-start | bytes 6148
  5.6 6.4 %collective-permute-start.3 = (bf16[2,16,128]{2,1,0:T(8,128)(2,1)S(1)}, bf16[2,16,128]{2,1,0:T(8,128)(2,1)S(1)}, u32[]{:S(2)}, u32[]{:S(2)}) collective-permute-start(bf16[2,16,128]{2,1,0:T(8,128)(2,1)S(1)} %shard_map.82.own_ref), channel_id=1, source_target_pairs={{0,8},{4,12},{8,0},{12,4},{1,9},{5,13},{9,1},{13,5},{2,10},{6,14},... | collective-permute-start | bytes 24584 | tf_op jit(solution)/shard_map/ppermute | solution.py:25
  8.3 5.4 %collective-permute-start.2 = (bf16[2,16,128]{2,1,0:T(8,128)(2,1)S(1)}, bf16[2,16,128]{2,1,0:T(8,128)(2,1)S(1)}, u32[]{:S(2)}, u32[]{:S(2)}) collective-permute-start(bf16[2,16,128]{2,1,0:T(8,128)(2,1)S(1)} %shard_map.82.own_ref), channel_id=1, source_target_pairs={{0,4},{4,8},{8,12},{12,0},{1,5},{5,9},{9,13},{13,1},{2,6},{6,10},{... | collective-permute-start | bytes 24584 | tf_op jit(solution)/shard_map/ppermute | solution.py:25

commit v2 on v1

v2 whole, which is shorter than its diff:
```python
import functools

import jax
import jax.numpy as jnp
from jax import lax
from jax.experimental import pallas as pl
from jax.experimental.pallas import tpu as pltpu
from jax.sharding import PartitionSpec as P

EPSILON = 1e-06
LANES = 128
VMEM = pl.BlockSpec(memory_space=pltpu.VMEM)
HBM = pl.BlockSpec(memory_space=pltpu.HBM)


def swapped(x, axis, first):
    count = lax.axis_size(axis)
    pairs = []
    for low in range(first, first + count, 2):
        a, b = low % count, (low + 1) % count
        pairs += [(a, b), (b, a)]
    return lax.ppermute(x, axis, pairs)


def shifted(x, axis, by):
    count = lax.axis_size(axis)
    return lax.ppermute(x, axis, [(i, (i + by) % count) for i in range(count)])


def in_hbm(x):
    return pltpu.with_memory_space_constraint(x, pltpu.HBM)


def copies_of(sources, targets, sems):
    return [pltpu.make_async_copy(s, t, sems.at[i]) for i, (s, t) in enumerate(zip(sources, targets))]


def stage_kernel(*refs):
    count = len(refs) // 2
    copies = copies_of(refs[:count], refs[count:-1], refs[-1])
    first = lax.axis_index("tm") == 0

    @pl.when(first)
    def _():
        for copy in copies[-2:]:
            copy.start()

    for copy in copies[:-2]:
        copy.start()
    for copy in copies[:-2]:
        copy.wait()

    @pl.when(first)
    def _():
        for copy in copies[-2:]:
            copy.wait()


def pack_kernel(odd_ref, even_ref, own_ref, packed_ref):
    space, count = lax.axis_index("space"), lax.axis_size("space")
    frames, rows, cols, width = own_ref.shape
    is_even = lax.rem(space, 2) == 0
    even, odd = even_ref[...], odd_ref[...]
    above = jnp.where(space > 0, jnp.where(is_even, odd, even), jnp.zeros_like(even))
    below = jnp.where(space < count - 1, jnp.where(is_even, even, odd), jnp.zeros_like(even))
    channel = lax.broadcasted_iota(jnp.int32, (width, LANES), 0)
    lane = lax.broadcasted_iota(jnp.int32, (width, LANES), 1)
    total = jnp.zeros((frames * cols, LANES), jnp.float32)
    for r, block in enumerate([x[:, r] for x in (above, own_ref[...], below) for r in range(rows)]):
        spread = (lane == channel + r * width).astype(own_ref.dtype)
        total += jnp.dot(block.reshape(frames * cols, width), spread, preferred_element_type=jnp.float32)
    packed_ref[...] = total.astype(own_ref.dtype).reshape(packed_ref.shape)


def column_shift(x, by, cols):
    groups = x.shape[0] // cols
    column = lax.broadcasted_iota(jnp.int32, (groups, cols, x.shape[1]), 1).reshape(x.shape)
    edge = 0 if by > 0 else cols - 1
    return jnp.where(column == edge, 0.0, pltpu.roll(x, by % x.shape[0], axis=0))


def entry(frames, w_in_ref, b_in_ref, gain_ref, rows, width):
    frame_total, cols, _ = frames.shape
    features = w_in_ref.shape[1]
    tall = rows + 2
    block = tall * cols
    reach = 3 * width
    flat = frames.astype(jnp.float32).reshape(frame_total * cols, LANES)
    lane = lax.broadcasted_iota(jnp.int32, flat.shape, 1)
    west, east = column_shift(flat, 1, cols), column_shift(flat, -1, cols)

    def window(x, r, at):
        return pltpu.roll(x, (at - r * width) % LANES, axis=1) if at != r * width else x

    def by_position(parts):
        parts = [x.astype(jnp.bfloat16).reshape(frame_total, cols, LANES) for x in parts]
        return jnp.stack(parts, axis=1).reshape(frame_total * block, LANES)

    pair = by_position([jnp.where(lane < reach, window(west, r, 0), window(flat, r, reach)) for r in range(tall)])
    later = jnp.concatenate([east[cols:], east[:cols]], axis=0)
    last = by_position([jnp.where(lane < reach, window(east, r, 0), window(later, r, reach)) for r in range(tall)])
    size = (frame_total - 2) * block
    left = [pair[a * block : a * block + size] for a in range(3)] + [last[:size], last[2 * block : 2 * block + size]]

    def taps(a, e):
        return [w_in_ref[((a * 3 + b) * 3 + e) * width : ((a * 3 + b) * 3 + e + 1) * width, :] for b in range(3)]

    gap = [jnp.zeros((LANES - 2 * reach, features), jnp.bfloat16)]
    right = []
    for a in range(3):
        right += taps(a, 0) + taps(a, 1) + gap
    right += taps(0, 2) + taps(1, 2) + gap
    right += taps(2, 2) + [jnp.zeros((LANES - reach, features), jnp.bfloat16)]
    hidden = jnp.dot(
        jnp.concatenate(left, axis=1), jnp.concatenate(right, axis=0), preferred_element_type=jnp.float32
    )
    hidden = hidden + b_in_ref[...][None, :]
    inverse = lax.rsqrt(jnp.mean(hidden * hidden, axis=1, keepdims=True) + EPSILON)
    half = hidden * inverse * (0.5 * gain_ref[...][None, :])
    return (half + half * jnp.tanh(half)).astype(jnp.bfloat16)


def own_part(active, w_time_ref):
    features = active.shape[1]
    block = active.shape[0] // 2
    early, late = active[:block], active[block:]
    left = jnp.concatenate(
        [jnp.concatenate([jnp.zeros_like(early), early], axis=1), jnp.concatenate([early, late], axis=1)], axis=0
    )
    return jnp.dot(left, w_time_ref[features:, :], preferred_element_type=jnp.float32)


def earlier_part(active, w_time_ref):
    features = active.shape[1]
    block = active.shape[0] // 2
    early, late = active[:block], active[block:]
    left = jnp.concatenate(
        [jnp.concatenate([early, late], axis=1), jnp.concatenate([late, jnp.zeros_like(late)], axis=1)], axis=0
    )
    return jnp.dot(left, w_time_ref[: 2 * features, :], preferred_element_type=jnp.float32)


def add_row_taps(w_up_ref, w_sum_ref):
    size = w_sum_ref.shape[0] // 2
    top, middle, bottom = (w_up_ref[b * size : (b + 1) * size, :].astype(jnp.float32) for b in range(3))
    w_sum_ref[:size, :] = (middle + bottom).astype(w_sum_ref.dtype)
    w_sum_ref[size:, :] = (top + middle).astype(w_sum_ref.dtype)


def upsample(timed, w_up_ref, w_sum_ref, b_up_ref, wide_ref, done_ref, rows, cols):
    space, space_count = lax.axis_index("space"), lax.axis_size("space")
    features = timed.shape[1] // 2
    tall = rows + 2
    frames = timed.shape[0] // (tall * cols)
    out_width = done_ref.shape[-1]
    timed = timed.astype(jnp.bfloat16)

    def timed_row(f, h, r):
        x = timed[(f * tall + r) * cols : (f * tall + r + 1) * cols, h * features : (h + 1) * features]
        if r == 0:
            x = jnp.where(space > 0, x, jnp.zeros_like(x))
        if r == tall - 1:
            x = jnp.where(space < space_count - 1, x, jnp.zeros_like(x))
        return x

    doubled = [[timed_row(f, h, r) for r in range(tall)] for f in range(frames) for h in range(2)]
    tap_size = 3 * out_width
    for p in range(2):
        left = jnp.concatenate(
            [jnp.concatenate([frame[r + p + k] for frame in doubled for r in range(rows)], axis=0) for k in range(2)], axis=1
        )
        sums = []
        for e in range(3):
            outer = w_up_ref[(2 * p * 3 + e) * out_width : (2 * p * 3 + e + 1) * out_width, :]
            inner = w_sum_ref[p * tap_size + e * out_width : p * tap_size + (e + 1) * out_width, :]
            tap = jnp.concatenate([inner, outer] if p else [outer, inner], axis=1)
            sums.append(lax.dot_general(left, tap, (((1,), (1,)), ((), ())), preferred_element_type=jnp.float32))
        middle = sums[1] + b_up_ref[...][None, :]
        even = column_shift(sums[0], 1, cols) + (middle + sums[2])
        odd = column_shift(sums[2], -1, cols) + (middle + sums[0])
        for q, x in enumerate((even, odd)):
            low = x[:, :LANES]
            high = jnp.concatenate([x[:, LANES:]] * (LANES // (out_width - LANES)), axis=1)
            for i in range(2 * frames * rows):
                at = (i // rows) * 2 * rows + 2 * (i % rows) + p
                wide_ref[0, at, pl.ds(q, cols, stride=2), :] = low[i * cols : (i + 1) * cols]
                wide_ref[1, at, pl.ds(q, cols, stride=2), :] = high[i * cols : (i + 1) * cols]
    whole = jnp.concatenate([wide_ref[0], wide_ref[1][:, :, : out_width - LANES]], axis=2)
    done_ref[...] = whole.astype(done_ref.dtype).reshape(done_ref.shape)


def send_out(done_ref, out_ref, sem):
    copy = pltpu.make_async_copy(done_ref, out_ref, sem)
    copy.start()
    copy.wait()


def first_kernel(
    own_ref, w_in_ref, b_in_ref, gain_ref, b_time_ref, b_up_ref, w_time_hbm, w_up_hbm, _w_time, _w_up,
    out_ref, w_time_ref, w_up_ref, w_sum_ref, wide_ref, done_ref, sems, *, rows, width,
):
    first = lax.axis_index("tm") == 0
    cols = own_ref.shape[1]

    @pl.when(first)
    def _():
        add_row_taps(w_up_ref, w_sum_ref)
        own = own_ref[...]
        active = entry(jnp.concatenate([jnp.zeros_like(own), own], axis=0), w_in_ref, b_in_ref, gain_ref, rows, width)
        timed = own_part(active, w_time_ref) + b_time_ref[...][None, :]
        upsample(timed, w_up_ref, w_sum_ref, b_up_ref, wide_ref, done_ref, rows, cols)
        send_out(done_ref, out_ref, sems.at[2])

    @pl.when(jnp.logical_not(first))
    def _():
        time_copy, up_copy = copies_of((w_time_hbm, w_up_hbm), (w_time_ref, w_up_ref), sems)
        up_copy.start()
        time_copy.start()
        up_copy.wait()
        add_row_taps(w_up_ref, w_sum_ref)
        time_copy.wait()


def own_kernel(own_ref, one_ref, w_in_ref, b_in_ref, gain_ref, b_time_ref, w_time_ref, timed_ref, *, rows, width):
    @pl.when(lax.axis_index("tm") > 0)
    def _():
        active = entry(jnp.concatenate([one_ref[...], own_ref[...]], axis=0), w_in_ref, b_in_ref, gain_ref, rows, width)
        timed_ref[...] = own_part(active, w_time_ref) + b_time_ref[...][None, :]


def last_kernel(
    one_ref, two_ref, timed_ref, w_in_ref, b_in_ref, gain_ref, b_up_ref, w_time_ref, w_up_ref, w_sum_ref, _out,
    out_ref, wide_ref, done_ref, sem, *, rows, width,
):
    time = lax.axis_index("tm")

    @pl.when(time > 0)
    def _():
        two = jnp.where(time > 1, two_ref[...], jnp.zeros_like(two_ref))
        active = entry(jnp.concatenate([two, one_ref[...]], axis=0), w_in_ref, b_in_ref, gain_ref, rows, width)
        timed = timed_ref[...] + earlier_part(active, w_time_ref)
        upsample(timed, w_up_ref, w_sum_ref, b_up_ref, wide_ref, done_ref, rows, one_ref.shape[1])
        send_out(done_ref, out_ref, sem)


def params(mib):
    return pltpu.CompilerParams(vmem_limit_bytes=mib * 1024 * 1024)


def shards(latent, w_in, b_in, gain_in, w_time, b_time, w_up, b_up):
    frames, rows, cols, width = latent.shape
    features = w_in.shape[-1]
    out_width = w_up.shape[-1]
    w_time = in_hbm(w_time.reshape(-1, w_time.shape[-1]))
    w_up = in_hbm(jnp.swapaxes(w_up, 2, 3).reshape(-1, w_up.shape[2]))
    large = [pltpu.VMEM(w.shape, w.dtype) for w in (w_time, w_up)]
    out_shape = (2 * frames, 2 * rows, 2 * cols, out_width)
    sizes = dict(rows=rows, width=width)

    even = swapped(latent, "space", 0)
    odd = swapped(latent, "space", 1)
    arrays = [in_hbm(x) for x in (w_in.reshape(-1, features), b_in, gain_in, b_time, b_up, latent)] + [w_time, w_up]
    w_in, b_in, gain_in, b_time, b_up, own, w_time_kept, w_up_kept = pl.pallas_call(
        stage_kernel,
        out_shape=[pltpu.VMEM(x.shape, x.dtype) for x in arrays],
        in_specs=[HBM] * len(arrays),
        out_specs=[VMEM] * len(arrays),
        scratch_shapes=[pltpu.SemaphoreType.DMA((len(arrays),))],
        compiler_params=params(1),
    )(*arrays)
    own = pl.pallas_call(
        pack_kernel,
        out_shape=pltpu.VMEM((frames, cols, LANES), latent.dtype),
        in_specs=[VMEM] * 3,
        out_specs=VMEM,
        compiler_params=params(1),
    )(odd, even, own)
    one = shifted(own, "tm", 1)
    two = shifted(own, "tm", 2)

    finish = [
        pltpu.VMEM((2, 2 * frames * 2 * rows, 2 * cols, LANES), jnp.float32),
        pltpu.VMEM(out_shape, jnp.bfloat16),
    ]
    out, w_time_kept, w_up_kept, w_sum = pl.pallas_call(
        functools.partial(first_kernel, **sizes),
        out_shape=[pltpu.HBM(out_shape, jnp.bfloat16)] + large + [pltpu.VMEM((6 * out_width, features), jnp.bfloat16)],
        in_specs=[VMEM] * 6 + [HBM] * 2 + [VMEM] * 2,
        out_specs=[HBM] + [VMEM] * 3,
        scratch_shapes=finish + [pltpu.SemaphoreType.DMA((3,))],
        input_output_aliases={8: 1, 9: 2},
        compiler_params=params(16),
    )(own, w_in, b_in, gain_in, b_time, b_up, w_time, w_up, w_time_kept, w_up_kept)
    timed = pl.pallas_call(
        functools.partial(own_kernel, **sizes),
        out_shape=pltpu.VMEM((frames * (rows + 2) * cols, 2 * features), jnp.float32),
        in_specs=[VMEM] * 7,
        out_specs=VMEM,
        compiler_params=params(16),
    )(own, one, w_in, b_in, gain_in, b_time, w_time_kept)
    return pl.pallas_call(
        functools.partial(last_kernel, **sizes),
        out_shape=pltpu.HBM(out_shape, jnp.bfloat16),
        in_specs=[VMEM] * 10 + [HBM],
        out_specs=HBM,
        scratch_shapes=finish + [pltpu.SemaphoreType.DMA],
        input_output_aliases={10: 0},
        compiler_params=params(16),
    )(one, two, timed, w_in, b_in, gain_in, b_up, w_time_kept, w_up_kept, w_sum, out)


def solution(mesh):
    in_specs = (P(("clips", "tm"), "space", None, None), P(), P(), P(), P(), P(), P(), P())
    out_specs = P(("clips", "tm"), "space", None, None)
    return jax.shard_map(shards, mesh=mesh, in_specs=in_specs, out_specs=out_specs, check_vma=False)
```

time: 17.2 us -> 12.2 us (0.71)
  the two profiles are of different devices: /device:TPU:0 before, /device:TPU:10 now
where the time goes in v2:
time: 12.2 us; the launch traced here: 12 us
  Pallas kernels  6.03 us (49%)
  starting transfers between devices  3.48 us (29%)
  waiting for transfers between devices  2.48 us (20%)
    ppermute x2, starting transfers between devices, shifted(): return lax.ppermute(x, axis, [(i, (i + by) % count) for i in range(count)])  2.83 us
    pallas_call x1, Pallas kernels, shards(): pl.pallas_call(functools.partial(last_kernel, **sizes), out_shape=pltpu.H...  2.22 us
    pallas_call x1, Pallas kernels, shards(): pl.pallas_call(functools.partial(first_kernel, **sizes), out_shape=[pltpu...  1.91 us
    ppermute x2, waiting for transfers between devices, swapped(): return lax.ppermute(x, axis, pairs)  1.83 us
    pallas_call x1, Pallas kernels, shards(): pl.pallas_call(stage_kernel, out_shape=[pltpu.VMEM(x.shape, x.dtype) for...  1.05 us
    pallas_call x1, Pallas kernels, shards(): pl.pallas_call(functools.partial(own_kernel, **sizes), out_shape=pltpu.VM...  0.73 us
    ppermute x2, waiting for transfers between devices, shifted(): return lax.ppermute(x, axis, [(i, (i + by) % count) for i in range(count)])  0.66 us
    ppermute x2, starting transfers between devices, swapped(): return lax.ppermute(x, axis, pairs)  0.65 us
  transfers between devices with their start and end apart: 4, of which 2 were waited for; matrix products, arithmetic and copies ran while one was open for 0% of the time, Pallas kernels for 31%

profile of v2, /device:TPU:10, one launch (start us, length us, event | category | flops | bytes accessed | tf_op | source)
XLA Modules:
  0.0 12.0 jit_solution(15088151879193161716)
XLA Ops:
  0.0 0.0 collective-permute-start
  0.0 0.6 %collective-permute-start.1 = (bf16[2,2,16,16]{3,2,1,0:T(8,128)(2,1)}, bf16[2,2,16,16]{3,2,1,0:T(8,128)(2,1)S(1)}, u32[]{:S(2)}, u32[]{:S(2)}) collective-permute-start(bf16[2,2,16,16]{3,2,1,0:T(8,128)(2,1)} %refs_5_.1), channel_id=1, source_target_pairs={{0,1},{1,0},{2,3},{3,2},{4,5},{5,4},{6,7},{7,6},{8,9},{9,8},{10,11... | collective-permute-start | bytes 6152 | tf_op jit(solution)/shard_map/ppermute | solution.py:22
  0.7 1.1 %shard_map.82 = (bf16[432,384]{1,0:T(8,128)(2,1)S(1)}, f32[384]{0:T(512)S(1)}, f32[384]{0:T(512)S(1)}, f32[768]{0:T(1024)S(1)}, f32[192]{0:T(256)S(1)}, /*index=...) custom-call(bf16[432,384]{1,0:T(8,128)(2,1)} %bitcast.9, f32[384]{0:T(512)} %refs_1_.1, ...), custom_call_target="tpu_custom_call" | custom-call | tf_op jit(solution)/shard_map/pallas_call | solution.py:263
  1.7 1.8 %collective-permute-done.odd_ref = bf16[2,2,16,16]{3,2,1,0:T(8,128)(2,1)S(1)} collective-permute-done((bf16[2,2,16,16]{3,2,1,0:T(8,128)(2,1)}, bf16[2,2,16,16]{3,2,1,0:T(8,128)(2,1)S(1)}, u32[]{:S(2)}, u32[]{:S(2)}) %collective-permute-start) | collective-permute-done | bytes 2080 | tf_op jit(solution)/shard_map/ppermute | solution.py:22
  3.5 0.0 collective-permute-done.1.even_ref
  3.5 0.1 %shard_map.83.own_ref = bf16[2,16,128]{2,1,0:T(8,128)(2,1)S(1)} custom-call(bf16[2,2,16,16]{3,2,1,0:T(8,128)(2,1)S(1)} %collective-permute-done.odd_ref, bf16[2,2,16,16]{3,2,1,0:T(8,128)(2,1)S(1)} %collective-permute-done.1.even_ref, bf16[2,2,16,16]{3,2,1,0:T(8,128)(2,1)S(1)} %get-tuple-element.17.own_ref), custom_call_target="tpu_custom_call" | custom-call | tf_op jit(solution)/shard_map/pallas_call | solution.py:271
  3.7 1.6 %collective-permute-start.2 = (bf16[2,16,128]{2,1,0:T(8,128)(2,1)S(1)}, bf16[2,16,128]{2,1,0:T(8,128)(2,1)S(1)}, u32[]{:S(2)}, u32[]{:S(2)}) collective-permute-start(bf16[2,16,128]{2,1,0:T(8,128)(2,1)S(1)} %shard_map.83.own_ref), channel_id=1, source_target_pairs={{0,4},{4,8},{8,12},{12,0},{1,5},{5,9},{9,13},{13,1},{2,6},{6,10},{... | collective-permute-start | bytes 24584 | tf_op jit(solution)/shard_map/ppermute | solution.py:27
  5.3 1.2 %collective-permute-start.3 = (bf16[2,16,128]{2,1,0:T(8,128)(2,1)S(1)}, bf16[2,16,128]{2,1,0:T(8,128)(2,1)S(1)}, u32[]{:S(2)}, u32[]{:S(2)}) collective-permute-start(bf16[2,16,128]{2,1,0:T(8,128)(2,1)S(1)} %shard_map.83.own_ref), channel_id=1, source_target_pairs={{0,8},{4,12},{8,0},{12,4},{1,9},{5,13},{9,1},{13,5},{2,10},{6,14},... | collective-permute-start | bytes 24584 | tf_op jit(solution)/shard_map/ppermute | solution.py:27
  6.5 1.9 %shard_map.84 = (bf16[4,4,32,192]{3,2,1,0:T(8,128)(2,1)}, bf16[1152,768]{1,0:T(8,128)(2,1)S(1)}, bf16[1728,384]{1,0:T(8,128)(2,1)S(1)}, bf16[1152,384]{1,0:T(8,128)(2,1)S(1)}) custom-call(bf16[2,16,128]{2,1,0:T(8,128)(2,1)S(1)} %shard_map.83.own_ref, bf16[432,384]{1,0:T(8,128)(2,1)S(1)} %get-tuple-element.18.w_in_ref, ...), custom_call_target="tpu_custom_call", output_to_operand_aliasing={{1}: (8, {}), {2}: (9, {})} | custom-call | tf_op jit(solution)/shard_map/pallas_call | solution.py:285
  8.4 0.0 collective-permute-done.2.one_ref
  8.4 0.7 %shard_map.85.timed_ref = f32[128,768]{1,0:T(8,128)S(1)} custom-call(bf16[2,16,128]{2,1,0:T(8,128)(2,1)S(1)} %shard_map.83.own_ref, bf16[2,16,128]{2,1,0:T(8,128)(2,1)S(1)} %collective-permute-done.2.one_ref, bf16[432,384]{1,0:T(8,128)(2,1)S(1)} %get-tuple-element.18.w_in_ref, f32[384]{0:T(512)S(1)} %get-tuple-element.19.b_in_ref, ...), custom_call_target="tpu_custom_call" | custom-call | tf_op jit(solution)/shard_map/pallas_call | solution.py:294
  9.2 0.7 %collective-permute-done.3.two_ref = bf16[2,16,128]{2,1,0:T(8,128)(2,1)S(1)} collective-permute-done((bf16[2,16,128]{2,1,0:T(8,128)(2,1)S(1)}, bf16[2,16,128]{2,1,0:T(8,128)(2,1)S(1)}, u32[]{:S(2)}, u32[]{:S(2)}) %collective-permute-start.3) | collective-permute-done | bytes 8224 | tf_op jit(solution)/shard_map/ppermute | solution.py:27
  9.8 2.2 %shard_map.86 = bf16[4,4,32,192]{3,2,1,0:T(8,128)(2,1)} custom-call(bf16[2,16,128]{2,1,0:T(8,128)(2,1)S(1)} %collective-permute-done.2.one_ref, bf16[2,16,128]{2,1,0:T(8,128)(2,1)S(1)} %collective-permute-done.3.two_ref, f32[128,768]{1,0:T(8,128)S(1)} %shard_map.85.timed_ref, ...), custom_call_target="tpu_custom_call", output_to_operand_aliasing={{}: (10, {})} | custom-call | tf_op jit(solution)/shard_map/pallas_call | solution.py:301
Async XLA Ops:
  0.0 3.5 %collective-permute-start = (bf16[2,2,16,16]{3,2,1,0:T(8,128)(2,1)}, bf16[2,2,16,16]{3,2,1,0:T(8,128)(2,1)S(1)}, u32[]{:S(2)}, u32[]{:S(2)}) collective-permute-start(bf16[2,2,16,16]{3,2,1,0:T(8,128)(2,1)} %refs_5_.1), channel_id=1, source_target_pairs={{1,2},{2,1},{3,0},{0,3},{5,6},{6,5},{7,4},{4,7},{9,10},{10,9},{11,... | collective-permute-start | bytes 6152 | tf_op jit(solution)/shard_map/ppermute | solution.py:22
  0.0 3.5 %collective-permute-start.1 = (bf16[2,2,16,16]{3,2,1,0:T(8,128)(2,1)}, bf16[2,2,16,16]{3,2,1,0:T(8,128)(2,1)S(1)}, u32[]{:S(2)}, u32[]{:S(2)}) collective-permute-start(bf16[2,2,16,16]{3,2,1,0:T(8,128)(2,1)} %refs_5_.1), channel_id=1, source_target_pairs={{0,1},{1,0},{2,3},{3,2},{4,5},{5,4},{6,7},{7,6},{8,9},{9,8},{10,11... | collective-permute-start | bytes 6152 | tf_op jit(solution)/shard_map/ppermute | solution.py:22
  3.7 4.8 %collective-permute-start.2 = (bf16[2,16,128]{2,1,0:T(8,128)(2,1)S(1)}, bf16[2,16,128]{2,1,0:T(8,128)(2,1)S(1)}, u32[]{:S(2)}, u32[]{:S(2)}) collective-permute-start(bf16[2,16,128]{2,1,0:T(8,128)(2,1)S(1)} %shard_map.83.own_ref), channel_id=1, source_target_pairs={{0,4},{4,8},{8,12},{12,0},{1,5},{5,9},{9,13},{13,1},{2,6},{6,10},{... | collective-permute-start | bytes 24584 | tf_op jit(solution)/shard_map/ppermute | solution.py:27
  5.3 4.5 %collective-permute-start.3 = (bf16[2,16,128]{2,1,0:T(8,128)(2,1)S(1)}, bf16[2,16,128]{2,1,0:T(8,128)(2,1)S(1)}, u32[]{:S(2)}, u32[]{:S(2)}) collective-permute-start(bf16[2,16,128]{2,1,0:T(8,128)(2,1)S(1)} %shard_map.83.own_ref), channel_id=1, source_target_pairs={{0,8},{4,12},{8,0},{12,4},{1,9},{5,13},{9,1},{13,5},{2,10},{6,14},... | collective-permute-start | bytes 24584 | tf_op jit(solution)/shard_map/ppermute | solution.py:27

commit v3 on v2

v3 whole, which is shorter than its diff:
```python
import functools

import jax
import jax.numpy as jnp
from jax import lax
from jax.experimental import pallas as pl
from jax.experimental.pallas import tpu as pltpu
from jax.sharding import PartitionSpec as P

EPSILON = 1e-06
LANES = 128
VMEM = pl.BlockSpec(memory_space=pltpu.VMEM)
HBM = pl.BlockSpec(memory_space=pltpu.HBM)


def swapped(x, axis, first):
    count = lax.axis_size(axis)
    pairs = []
    for low in range(first, first + count, 2):
        a, b = low % count, (low + 1) % count
        pairs += [(a, b), (b, a)]
    return lax.ppermute(x, axis, pairs)


def shifted(x, axis, by):
    count = lax.axis_size(axis)
    return lax.ppermute(x, axis, [(i, (i + by) % count) for i in range(count)])


def in_hbm(x):
    return pltpu.with_memory_space_constraint(x, pltpu.HBM)


def copies_of(sources, targets, sems):
    return [pltpu.make_async_copy(s, t, sems.at[i]) for i, (s, t) in enumerate(zip(sources, targets))]


def stage_kernel(*refs):
    count = len(refs) // 2
    copies = copies_of(refs[:count], refs[count:-1], refs[-1])
    early = lax.axis_index("tm") <= 1

    @pl.when(early)
    def _():
        for copy in copies[-2:]:
            copy.start()

    for copy in copies[:-2]:
        copy.start()
    for copy in copies[:-2]:
        copy.wait()

    @pl.when(early)
    def _():
        for copy in copies[-2:]:
            copy.wait()


def pack_kernel(odd_ref, even_ref, own_ref, w_up_ref, packed_ref, taps_ref):
    time = lax.axis_index("tm")
    space, count = lax.axis_index("space"), lax.axis_size("space")
    frames, rows, cols, width = own_ref.shape
    is_even = lax.rem(space, 2) == 0
    even, odd = even_ref[...], odd_ref[...]
    above = jnp.where(space > 0, jnp.where(is_even, odd, even), jnp.zeros_like(even))
    below = jnp.where(space < count - 1, jnp.where(is_even, even, odd), jnp.zeros_like(even))
    channel = lax.broadcasted_iota(jnp.int32, (width, LANES), 0)
    lane = lax.broadcasted_iota(jnp.int32, (width, LANES), 1)
    total = jnp.zeros((frames * cols, LANES), jnp.float32)
    for r, block in enumerate([x[:, r] for x in (above, own_ref[...], below) for r in range(rows)]):
        spread = (lane == channel + r * width).astype(own_ref.dtype)
        total += jnp.dot(block.reshape(frames * cols, width), spread, preferred_element_type=jnp.float32)
    packed_ref[...] = total.astype(own_ref.dtype).reshape(packed_ref.shape)

    @pl.when(time == 0)
    def _():
        prepare_taps(w_up_ref, taps_ref)


def column_shift(x, by, cols):
    groups = x.shape[0] // cols
    column = lax.broadcasted_iota(jnp.int32, (groups, cols, x.shape[1]), 1).reshape(x.shape)
    edge = 0 if by > 0 else cols - 1
    return jnp.where(column == edge, 0.0, pltpu.roll(x, by % x.shape[0], axis=0))


def column_taps(frames, rows, width):
    frame_total, cols, _ = frames.shape
    tall = rows + 2
    reach = 3 * width
    flat = frames.astype(jnp.float32).reshape(frame_total * cols, LANES)
    lane = lax.broadcasted_iota(jnp.int32, flat.shape, 1)
    west, east = column_shift(flat, 1, cols), column_shift(flat, -1, cols)
    later = jnp.concatenate([east[cols:], east[:cols]], axis=0)

    def window(x, r, at):
        return pltpu.roll(x, (at - r * width) % LANES, axis=1) if at != r * width else x

    def by_position(x, y):
        parts = [jnp.where(lane < reach, window(x, r, 0), window(y, r, reach)) for r in range(tall)]
        parts = [part.astype(jnp.bfloat16).reshape(frame_total, cols, LANES) for part in parts]
        return jnp.stack(parts, axis=1).reshape(frame_total * tall * cols, LANES)

    return by_position(west, flat), by_position(east, later)


def weight_taps(w_in_ref, width, taps):
    rows = [
        w_in_ref[((a * 3 + b) * 3 + e) * width : ((a * 3 + b) * 3 + e + 1) * width, :] for a, e in taps for b in range(3)
    ]
    return rows + [jnp.zeros((LANES - len(rows) * width, w_in_ref.shape[1]), jnp.bfloat16)]


def entry(frames, w_in_ref, b_in_ref, rows, width):
    pair, last = column_taps(frames, rows, width)
    block = (rows + 2) * frames.shape[1]
    size = (frames.shape[0] - 2) * block
    left = [pair[a * block : a * block + size] for a in range(3)] + [last[:size], last[2 * block : 2 * block + size]]
    right = []
    for taps in [[(a, 0), (a, 1)] for a in range(3)] + [[(0, 2), (1, 2)], [(2, 2)]]:
        right += weight_taps(w_in_ref, width, taps)
    left, right = jnp.concatenate(left, axis=1), jnp.concatenate(right, axis=0)
    return jnp.dot(left, right, preferred_element_type=jnp.float32) + b_in_ref[...][None, :]


def entry_of_two(frames, w_in_ref, rows, width):
    pair, last = column_taps(jnp.concatenate([frames, jnp.zeros_like(frames[:1])], axis=0), rows, width)
    block = (rows + 2) * frames.shape[1]
    left = [pair[: 2 * block], pair[block:], last[: 2 * block]]
    right = []
    for taps in ([(0, 0), (0, 1)], [(1, 0), (1, 1)], [(0, 2), (1, 2)]):
        right += weight_taps(w_in_ref, width, taps)
    left, right = jnp.concatenate(left, axis=1), jnp.concatenate(right, axis=0)
    return jnp.dot(left, right, preferred_element_type=jnp.float32)


def normalized(hidden, gain_ref):
    inverse = lax.rsqrt(jnp.mean(hidden * hidden, axis=1, keepdims=True) + EPSILON)
    half = hidden * inverse * (0.5 * gain_ref[...][None, :])
    return (half + half * jnp.tanh(half)).astype(jnp.bfloat16)


def own_part(active, w_time_ref):
    features = active.shape[1]
    block = active.shape[0] // 2
    early, late = active[:block], active[block:]
    left = jnp.concatenate(
        [jnp.concatenate([jnp.zeros_like(early), early], axis=1), jnp.concatenate([early, late], axis=1)], axis=0
    )
    return jnp.dot(left, w_time_ref[features:, :], preferred_element_type=jnp.float32)


def earlier_part(active, w_time_ref):
    features = active.shape[1]
    block = active.shape[0] // 2
    early, late = active[:block], active[block:]
    left = jnp.concatenate(
        [jnp.concatenate([early, late], axis=1), jnp.concatenate([late, jnp.zeros_like(late)], axis=1)], axis=0
    )
    return jnp.dot(left, w_time_ref[: 2 * features, :], preferred_element_type=jnp.float32)


def prepare_taps(w_up_ref, taps_ref):
    features = w_up_ref.shape[1]
    out_width = taps_ref.shape[-1]
    for e in range(3):
        taps = [w_up_ref[(b * 3 + e) * out_width : (b * 3 + e + 1) * out_width, :].T for b in range(3)]
        top, middle, bottom = (x.astype(jnp.float32) for x in taps)
        taps_ref[0, e, :features] = taps[0]
        taps_ref[0, e, features:] = (middle + bottom).astype(taps_ref.dtype)
        taps_ref[1, e, :features] = (top + middle).astype(taps_ref.dtype)
        taps_ref[1, e, features:] = taps[2]


def upsample(timed, taps_ref, b_up_ref, out_ref, wide_ref, done_ref, sems, rows, cols):
    space, space_count = lax.axis_index("space"), lax.axis_size("space")
    features = timed.shape[1] // 2
    tall = rows + 2
    frames = timed.shape[0] // (tall * cols)
    out_width = done_ref.shape[-1]
    timed = timed.astype(jnp.bfloat16)

    def timed_row(f, h, r):
        x = timed[(f * tall + r) * cols : (f * tall + r + 1) * cols, h * features : (h + 1) * features]
        if r == 0:
            x = jnp.where(space > 0, x, jnp.zeros_like(x))
        if r == tall - 1:
            x = jnp.where(space < space_count - 1, x, jnp.zeros_like(x))
        return x

    doubled = [[timed_row(f, h, r) for r in range(tall)] for f in range(frames) for h in range(2)]
    copies = []
    for p in range(2):
        left = jnp.concatenate(
            [jnp.concatenate([frame[r + p + k] for frame in doubled for r in range(rows)], axis=0) for k in range(2)], axis=1
        )
        sums = [jnp.dot(left, taps_ref[p, e], preferred_element_type=jnp.float32) for e in range(3)]
        middle = sums[1] + b_up_ref[...][None, :]
        even = column_shift(sums[0], 1, cols) + (middle + sums[2])
        odd = column_shift(sums[2], -1, cols) + (middle + sums[0])
        half = even.shape[0]
        for q, x in enumerate((even, odd)):
            wide_ref[p, 0, pl.ds(q, half, stride=2), :] = x[:, :LANES]
            wide_ref[p, 1, pl.ds(q, half, stride=2), pl.ds(0, out_width - LANES)] = x[:, LANES:]
        low, high = wide_ref[p, 0], wide_ref[p, 1, :, pl.ds(0, out_width - LANES)]
        place = done_ref.shape[1:-1]
        done_ref[p, :, :, :, :LANES] = low.astype(done_ref.dtype).reshape(place + (LANES,))
        done_ref[p, :, :, :, LANES:] = high.astype(done_ref.dtype).reshape(place + (out_width - LANES,))
        copies.append(pltpu.make_async_copy(done_ref.at[p], out_ref.at[:, :, p], sems.at[p]))
        copies[-1].start()
    for copy in copies:
        copy.wait()


def first_kernel(
    own_ref, w_in_ref, b_in_ref, gain_ref, b_time_ref, b_up_ref, w_time_hbm, w_up_hbm, _w_time, _w_up, _taps,
    out_ref, w_time_ref, w_up_ref, taps_ref, wide_ref, done_ref, sems, *, rows, width,
):
    time = lax.axis_index("tm")

    @pl.when(time == 0)
    def _():
        own = own_ref[...]
        hidden = entry(jnp.concatenate([jnp.zeros_like(own), own], axis=0), w_in_ref, b_in_ref, rows, width)
        timed = own_part(normalized(hidden, gain_ref), w_time_ref) + b_time_ref[...][None, :]
        upsample(timed, taps_ref, b_up_ref, out_ref, wide_ref, done_ref, sems, rows, own.shape[1])

    @pl.when(time > 1)
    def _():
        time_copy, up_copy = copies_of((w_time_hbm, w_up_hbm), (w_time_ref, w_up_ref), sems)
        up_copy.start()
        time_copy.start()
        up_copy.wait()
        prepare_taps(w_up_ref, taps_ref)
        time_copy.wait()

    @pl.when(time == 1)
    def _():
        prepare_taps(w_up_ref, taps_ref)


def middle_kernel(
    own_ref, one_ref, w_in_ref, b_in_ref, gain_ref, b_time_ref, b_up_ref, w_time_ref, taps_ref, _out,
    out_ref, hidden_ref, timed_ref, wide_ref, done_ref, sems, *, rows, width,
):
    time = lax.axis_index("tm")
    size = hidden_ref.shape[0]

    def known():
        frames = jnp.concatenate([jnp.zeros_like(one_ref), one_ref[...], own_ref[...]], axis=0)
        return entry(frames, w_in_ref, b_in_ref, rows, width)

    @pl.when(time == 1)
    def _():
        active = normalized(known(), gain_ref)
        timed = own_part(active[size:], w_time_ref) + earlier_part(active[:size], w_time_ref) + b_time_ref[...][None, :]
        upsample(timed, taps_ref, b_up_ref, out_ref, wide_ref, done_ref, sems, rows, own_ref.shape[1])

    @pl.when(time > 1)
    def _():
        hidden = known()
        hidden_ref[...] = hidden[:size]
        timed_ref[...] = own_part(normalized(hidden[size:], gain_ref), w_time_ref) + b_time_ref[...][None, :]


def last_kernel(
    two_ref, hidden_ref, timed_ref, w_in_ref, gain_ref, b_up_ref, w_time_ref, taps_ref, _out,
    out_ref, wide_ref, done_ref, sems, *, rows, width,
):
    @pl.when(lax.axis_index("tm") > 1)
    def _():
        active = normalized(hidden_ref[...] + entry_of_two(two_ref[...], w_in_ref, rows, width), gain_ref)
        timed = timed_ref[...] + earlier_part(active, w_time_ref)
        upsample(timed, taps_ref, b_up_ref, out_ref, wide_ref, done_ref, sems, rows, two_ref.shape[1])


def params(mib):
    return pltpu.CompilerParams(vmem_limit_bytes=mib * 1024 * 1024)


def shards(latent, w_in, b_in, gain_in, w_time, b_time, w_up, b_up):
    frames, rows, cols, width = latent.shape
    features = w_in.shape[-1]
    out_width = w_up.shape[-1]
    w_time = in_hbm(w_time.reshape(-1, w_time.shape[-1]))
    w_up = in_hbm(jnp.swapaxes(w_up, 2, 3).reshape(-1, w_up.shape[2]))
    out_shape = (2 * frames, rows, 2, 2 * cols, out_width)

    even = swapped(latent, "space", 0)
    odd = swapped(latent, "space", 1)
    arrays = [in_hbm(x) for x in (w_in.reshape(-1, features), b_in, gain_in, b_time, b_up, latent)] + [w_time, w_up]
    w_in, b_in, gain_in, b_time, b_up, own, w_time_kept, w_up_kept = pl.pallas_call(
        stage_kernel,
        out_shape=[pltpu.VMEM(x.shape, x.dtype) for x in arrays],
        in_specs=[HBM] * len(arrays),
        out_specs=[VMEM] * len(arrays),
        scratch_shapes=[pltpu.SemaphoreType.DMA((len(arrays),))],
        compiler_params=params(1),
    )(*arrays)
    positions = frames * (rows + 2) * cols
    timed_shape = pltpu.VMEM((positions, 2 * features), jnp.float32)
    taps_shape = pltpu.VMEM((2, 3, 2 * features, out_width), jnp.bfloat16)
    own, taps = pl.pallas_call(
        pack_kernel,
        out_shape=[pltpu.VMEM((frames, cols, LANES), latent.dtype), taps_shape],
        in_specs=[VMEM] * 4,
        out_specs=[VMEM] * 2,
        compiler_params=params(4),
    )(odd, even, own, w_up_kept)
    one = shifted(own, "tm", 1)
    two = shifted(own, "tm", 2)

    finish = [
        pltpu.VMEM((2, 2, 2 * frames * rows * 2 * cols, LANES), jnp.float32),
        pltpu.VMEM((2, 2 * frames, rows, 2 * cols, out_width), jnp.bfloat16),
        pltpu.SemaphoreType.DMA((2,)),
    ]
    result = pltpu.HBM(out_shape, jnp.bfloat16)
    out, w_time_kept, w_up_kept, taps = pl.pallas_call(
        functools.partial(first_kernel, rows=rows, width=width),
        out_shape=[result] + [pltpu.VMEM(w.shape, w.dtype) for w in (w_time, w_up)] + [taps_shape],
        in_specs=[VMEM] * 6 + [HBM] * 2 + [VMEM] * 3,
        out_specs=[HBM] + [VMEM] * 3,
        scratch_shapes=finish,
        input_output_aliases={8: 1, 9: 2, 10: 3},
        compiler_params=params(16),
    )(own, w_in, b_in, gain_in, b_time, b_up, w_time, w_up, w_time_kept, w_up_kept, taps)
    out, hidden, timed = pl.pallas_call(
        functools.partial(middle_kernel, rows=rows, width=width),
        out_shape=[result, pltpu.VMEM((positions, features), jnp.float32), timed_shape],
        in_specs=[VMEM] * 9 + [HBM],
        out_specs=[HBM, VMEM, VMEM],
        scratch_shapes=finish,
        input_output_aliases={9: 0},
        compiler_params=params(16),
    )(own, one, w_in, b_in, gain_in, b_time, b_up, w_time_kept, taps, out)
    out = pl.pallas_call(
        functools.partial(last_kernel, rows=rows, width=width),
        out_shape=pltpu.HBM(out_shape, jnp.bfloat16),
        in_specs=[VMEM] * 8 + [HBM],
        out_specs=HBM,
        scratch_shapes=finish,
        input_output_aliases={8: 0},
        compiler_params=params(16),
    )(two, hidden, timed, w_in, gain_in, b_up, w_time_kept, taps, out)
    return out.reshape(2 * frames, 2 * rows, 2 * cols, out_width)


def solution(mesh):
    in_specs = (P(("clips", "tm"), "space", None, None), P(), P(), P(), P(), P(), P(), P())
    out_specs = P(("clips", "tm"), "space", None, None)
    return jax.shard_map(shards, mesh=mesh, in_specs=in_specs, out_specs=out_specs, check_vma=False)
```

time: 12.2 us -> 11.8 us (0.967)
  the two profiles are of different devices: /device:TPU:10 before, /device:TPU:18 now
where the time goes in v3:
time: 11.8 us; the launch traced here: 11.7 us
  Pallas kernels  5.81 us (49%)
  waiting for transfers between devices  3.22 us (27%)
  starting transfers between devices  2.58 us (22%)
    pallas_call x1, Pallas kernels, shards(): pl.pallas_call(functools.partial(first_kernel, rows=rows, width=width), o...  1.95 us
    ppermute x2, starting transfers between devices, shifted(): return lax.ppermute(x, axis, [(i, (i + by) % count) for i in range(count)])  1.93 us
    pallas_call x1, Pallas kernels, shards(): pl.pallas_call(functools.partial(last_kernel, rows=rows, width=width), ou...  1.84 us
    ppermute x2, waiting for transfers between devices, swapped(): return lax.ppermute(x, axis, pairs)  1.83 us
    ppermute x2, waiting for transfers between devices, shifted(): return lax.ppermute(x, axis, [(i, (i + by) % count) for i in range(count)])  1.4 us
    pallas_call x1, Pallas kernels, shards(): pl.pallas_call(stage_kernel, out_shape=[pltpu.VMEM(x.shape, x.dtype) for...  1.05 us
    pallas_call x1, Pallas kernels, shards(): pl.pallas_call(functools.partial(middle_kernel, rows=rows, width=width),...  0.84 us
    ppermute x2, starting transfers between devices, swapped(): return lax.ppermute(x, axis, pairs)  0.65 us
  transfers between devices with their start and end apart: 4, of which 2 were waited for; matrix products, arithmetic and copies ran while one was open for 0% of the time, Pallas kernels for 33%

profile of v3, /device:TPU:18, one launch (start us, length us, event | category | flops | bytes accessed | tf_op | source)
XLA Modules:
  0.0 11.7 jit_solution(15317593793387206520)
XLA Ops:
  0.0 0.0 collective-permute-start
  0.0 0.6 %collective-permute-start.1 = (bf16[2,2,16,16]{3,2,1,0:T(8,128)(2,1)}, bf16[2,2,16,16]{3,2,1,0:T(8,128)(2,1)S(1)}, u32[]{:S(2)}, u32[]{:S(2)}) collective-permute-start(bf16[2,2,16,16]{3,2,1,0:T(8,128)(2,1)} %refs_5_.1), channel_id=1, source_target_pairs={{0,1},{1,0},{2,3},{3,2},{4,5},{5,4},{6,7},{7,6},{8,9},{9,8},{10,11... | collective-permute-start | bytes 6152 | tf_op jit(solution)/shard_map/ppermute | solution.py:22
  0.7 1.1 %shard_map.82 = (bf16[432,384]{1,0:T(8,128)(2,1)S(1)}, f32[384]{0:T(512)S(1)}, f32[384]{0:T(512)S(1)}, f32[768]{0:T(1024)S(1)}, f32[192]{0:T(256)S(1)}, /*index=...) custom-call(bf16[432,384]{1,0:T(8,128)(2,1)} %bitcast.10, f32[384]{0:T(512)} %refs_1_.1, ...), custom_call_target="tpu_custom_call" | custom-call | tf_op jit(solution)/shard_map/pallas_call | solution.py:292
  1.7 1.8 %collective-permute-done.odd_ref = bf16[2,2,16,16]{3,2,1,0:T(8,128)(2,1)S(1)} collective-permute-done((bf16[2,2,16,16]{3,2,1,0:T(8,128)(2,1)}, bf16[2,2,16,16]{3,2,1,0:T(8,128)(2,1)S(1)}, u32[]{:S(2)}, u32[]{:S(2)}) %collective-permute-start) | collective-permute-done | bytes 2080 | tf_op jit(solution)/shard_map/ppermute | solution.py:22
  3.5 0.0 collective-permute-done.1.even_ref
  3.5 0.1 %shard_map.83 = (bf16[2,16,128]{2,1,0:T(8,128)(2,1)S(1)}, bf16[2,3,768,192]{3,2,1,0:T(8,128)(2,1)S(1)}) custom-call(bf16[2,2,16,16]{3,2,1,0:T(8,128)(2,1)S(1)} %collective-permute-done.odd_ref, bf16[2,2,16,16]{3,2,1,0:T(8,128)(2,1)S(1)} %collective-permute-done.1.even_ref, bf16[2,2,16,16]{3,2,1,0:T(8,128)(2,1)S(1)} %get-tuple-element.21.own_ref, ...), custom_call_target="tpu_custom_call" | custom-call | tf_op jit(solution)/shard_map/pallas_call | solution.py:303
  3.7 1.6 %collective-permute-start.3 = (bf16[2,16,128]{2,1,0:T(8,128)(2,1)S(1)}, bf16[2,16,128]{2,1,0:T(8,128)(2,1)S(1)}, u32[]{:S(2)}, u32[]{:S(2)}) collective-permute-start(bf16[2,16,128]{2,1,0:T(8,128)(2,1)S(1)} %get-tuple-element.23.own_ref), channel_id=1, source_target_pairs={{0,4},{4,8},{8,12},{12,0},{1,5},{5,9},{9,13},{13,1},{2,6},{6,10},{... | collective-permute-start | bytes 24584 | tf_op jit(solution)/shard_map/ppermute | solution.py:27
  5.3 0.3 %collective-permute-start.2 = (bf16[2,16,128]{2,1,0:T(8,128)(2,1)S(1)}, bf16[2,16,128]{2,1,0:T(8,128)(2,1)S(1)}, u32[]{:S(2)}, u32[]{:S(2)}) collective-permute-start(bf16[2,16,128]{2,1,0:T(8,128)(2,1)S(1)} %get-tuple-element.23.own_ref), channel_id=1, source_target_pairs={{0,8},{4,12},{8,0},{12,4},{1,9},{5,13},{9,1},{13,5},{2,10},{6,14},... | collective-permute-start | bytes 24584 | tf_op jit(solution)/shard_map/ppermute | solution.py:27
  5.6 1.9 %shard_map.84 = (bf16[4,2,2,32,192]{4,3,2,1,0:T(8,128)(2,1)}, bf16[1152,768]{1,0:T(8,128)(2,1)S(1)}, bf16[1728,384]{1,0:T(8,128)(2,1)S(1)}, bf16[2,3,768,192]{3,2,1,0:T(8,128)(2,1)S(1)}) custom-call(bf16[2,16,128]{2,1,0:T(8,128)(2,1)S(1)} %get-tuple-element.23.own_ref, ...), custom_call_target="tpu_custom_call", output_to_operand_aliasing={{1}: (8, {}), {2}: (9, {}), {3}: (10, {})} | custom-call | tf_op jit(solution)/shard_map/pallas_call | solution.py:319
  7.6 0.0 collective-permute-done.3.one_ref
  7.6 0.8 %shard_map.85 = (bf16[4,2,2,32,192]{4,3,2,1,0:T(8,128)(2,1)}, f32[128,384]{1,0:T(8,128)S(1)}, f32[128,768]{1,0:T(8,128)S(1)}) custom-call(bf16[2,16,128]{2,1,0:T(8,128)(2,1)S(1)} %get-tuple-element.23.own_ref, bf16[2,16,128]{2,1,0:T(8,128)(2,1)S(1)} %collective-permute-done.3.one_ref, ...), custom_call_target="tpu_custom_call", output_to_operand_aliasing={{0}: (9, {})} | custom-call | tf_op jit(solution)/shard_map/pallas_call | solution.py:328
  8.4 1.4 %collective-permute-done.2.two_ref = bf16[2,16,128]{2,1,0:T(8,128)(2,1)S(1)} collective-permute-done((bf16[2,16,128]{2,1,0:T(8,128)(2,1)S(1)}, bf16[2,16,128]{2,1,0:T(8,128)(2,1)S(1)}, u32[]{:S(2)}, u32[]{:S(2)}) %collective-permute-start.2) | collective-permute-done | bytes 8224 | tf_op jit(solution)/shard_map/ppermute | solution.py:27
  9.8 1.8 %shard_map.86 = bf16[4,2,2,32,192]{4,3,2,1,0:T(8,128)(2,1)} custom-call(bf16[2,16,128]{2,1,0:T(8,128)(2,1)S(1)} %collective-permute-done.2.two_ref, f32[128,384]{1,0:T(8,128)S(1)} %get-tuple-element.34.hidden_ref, f32[128,768]{1,0:T(8,128)S(1)} %get-tuple-element.35.timed_ref, ...), custom_call_target="tpu_custom_call", output_to_operand_aliasing={{}: (8, {})} | custom-call | tf_op jit(solution)/shard_map/pallas_call | solution.py:337
Async XLA Ops:
  0.0 3.5 %collective-permute-start = (bf16[2,2,16,16]{3,2,1,0:T(8,128)(2,1)}, bf16[2,2,16,16]{3,2,1,0:T(8,128)(2,1)S(1)}, u32[]{:S(2)}, u32[]{:S(2)}) collective-permute-start(bf16[2,2,16,16]{3,2,1,0:T(8,128)(2,1)} %refs_5_.1), channel_id=1, source_target_pairs={{1,2},{2,1},{3,0},{0,3},{5,6},{6,5},{7,4},{4,7},{9,10},{10,9},{11,... | collective-permute-start | bytes 6152 | tf_op jit(solution)/shard_map/ppermute | solution.py:22
  0.0 3.5 %collective-permute-start.1 = (bf16[2,2,16,16]{3,2,1,0:T(8,128)(2,1)}, bf16[2,2,16,16]{3,2,1,0:T(8,128)(2,1)S(1)}, u32[]{:S(2)}, u32[]{:S(2)}) collective-permute-start(bf16[2,2,16,16]{3,2,1,0:T(8,128)(2,1)} %refs_5_.1), channel_id=1, source_target_pairs={{0,1},{1,0},{2,3},{3,2},{4,5},{5,4},{6,7},{7,6},{8,9},{9,8},{10,11... | collective-permute-start | bytes 6152 | tf_op jit(solution)/shard_map/ppermute | solution.py:22
  3.7 3.9 %collective-permute-start.3 = (bf16[2,16,128]{2,1,0:T(8,128)(2,1)S(1)}, bf16[2,16,128]{2,1,0:T(8,128)(2,1)S(1)}, u32[]{:S(2)}, u32[]{:S(2)}) collective-permute-start(bf16[2,16,128]{2,1,0:T(8,128)(2,1)S(1)} %get-tuple-element.23.own_ref), channel_id=1, source_target_pairs={{0,4},{4,8},{8,12},{12,0},{1,5},{5,9},{9,13},{13,1},{2,6},{6,10},{... | collective-permute-start | bytes 24584 | tf_op jit(solution)/shard_map/ppermute | solution.py:27
  5.3 4.5 %collective-permute-start.2 = (bf16[2,16,128]{2,1,0:T(8,128)(2,1)S(1)}, bf16[2,16,128]{2,1,0:T(8,128)(2,1)S(1)}, u32[]{:S(2)}, u32[]{:S(2)}) collective-permute-start(bf16[2,16,128]{2,1,0:T(8,128)(2,1)S(1)} %get-tuple-element.23.own_ref), channel_id=1, source_target_pairs={{0,8},{4,12},{8,0},{12,4},{1,9},{5,13},{9,1},{13,5},{2,10},{6,14},... | collective-permute-start | bytes 24584 | tf_op jit(solution)/shard_map/ppermute | solution.py:27

commit v4 on v3

--- a/solution.py
+++ b/solution.py
@@ -22,9 +22,14 @@
     return lax.ppermute(x, axis, pairs)
 
 
-def shifted(x, axis, by):
-    count = lax.axis_size(axis)
-    return lax.ppermute(x, axis, [(i, (i + by) % count) for i in range(count)])
+def moved(x, target_of):
+    times, spaces = lax.axis_size("tm"), lax.axis_size("space")
+    pairs = []
+    for t in range(times):
+        target = target_of(t)
+        for s in range(spaces):
+            pairs.append((t * spaces + s, target * spaces + (s if target > t else s ^ 1)))
+    return lax.ppermute(x, ("tm", "space"), pairs)
 
 
 def in_hbm(x):
@@ -42,22 +47,19 @@
 
     @pl.when(early)
     def _():
-        for copy in copies[-2:]:
-            copy.start()
-
-    for copy in copies[:-2]:
+        copies[-1].start()
+
+    for copy in copies[:-1]:
         copy.start()
-    for copy in copies[:-2]:
+    for copy in copies[:-1]:
         copy.wait()
 
     @pl.when(early)
     def _():
-        for copy in copies[-2:]:
-            copy.wait()
-
-
-def pack_kernel(odd_ref, even_ref, own_ref, w_up_ref, packed_ref, taps_ref):
-    time = lax.axis_index("tm")
+        copies[-1].wait()
+
+
+def pack_kernel(odd_ref, even_ref, own_ref, packed_ref):
     space, count = lax.axis_index("space"), lax.axis_size("space")
     frames, rows, cols, width = own_ref.shape
     is_even = lax.rem(space, 2) == 0
@@ -72,10 +74,6 @@
         total += jnp.dot(block.reshape(frames * cols, width), spread, preferred_element_type=jnp.float32)
     packed_ref[...] = total.astype(own_ref.dtype).reshape(packed_ref.shape)
 
-    @pl.when(time == 0)
-    def _():
-        prepare_taps(w_up_ref, taps_ref)
-
 
 def column_shift(x, by, cols):
     groups = x.shape[0] // cols
@@ -123,17 +121,6 @@
     return jnp.dot(left, right, preferred_element_type=jnp.float32) + b_in_ref[...][None, :]
 
 
-def entry_of_two(frames, w_in_ref, rows, width):
-    pair, last = column_taps(jnp.concatenate([frames, jnp.zeros_like(frames[:1])], axis=0), rows, width)
-    block = (rows + 2) * frames.shape[1]
-    left = [pair[: 2 * block], pair[block:], last[: 2 * block]]
-    right = []
-    for taps in ([(0, 0), (0, 1)], [(1, 0), (1, 1)], [(0, 2), (1, 2)]):
-        right += weight_taps(w_in_ref, width, taps)
-    left, right = jnp.concatenate(left, axis=1), jnp.concatenate(right, axis=0)
-    return jnp.dot(left, right, preferred_element_type=jnp.float32)
-
-
 def normalized(hidden, gain_ref):
     inverse = lax.rsqrt(jnp.mean(hidden * hidden, axis=1, keepdims=True) + EPSILON)
     half = hidden * inverse * (0.5 * gain_ref[...][None, :])
@@ -150,14 +137,13 @@
     return jnp.dot(left, w_time_ref[features:, :], preferred_element_type=jnp.float32)
 
 
-def earlier_part(active, w_time_ref):
-    features = active.shape[1]
-    block = active.shape[0] // 2
-    early, late = active[:block], active[block:]
-    left = jnp.concatenate(
-        [jnp.concatenate([early, late], axis=1), jnp.concatenate([late, jnp.zeros_like(late)], axis=1)], axis=0
-    )
-    return jnp.dot(left, w_time_ref[: 2 * features, :], preferred_element_type=jnp.float32)
+def finish(frames, w_in_ref, b_in_ref, gain_ref, b_time_ref, b_up_ref, w_time_ref, taps_ref, out_ref, scratch, rows, width):
+    cols = frames.shape[1]
+    active = normalized(entry(frames, w_in_ref, b_in_ref, rows, width), gain_ref)
+    block = (rows + 2) * cols
+    left = jnp.concatenate([active[a * block : (a + 2) * block] for a in range(3)], axis=1)
+    timed = jnp.dot(left, w_time_ref[...], preferred_element_type=jnp.float32) + b_time_ref[...][None, :]
+    upsample(timed, taps_ref, b_up_ref, out_ref, *scratch, rows, cols)
 
 
 def prepare_taps(w_up_ref, taps_ref):
@@ -213,13 +199,14 @@
 
 
 def first_kernel(
-    own_ref, w_in_ref, b_in_ref, gain_ref, b_time_ref, b_up_ref, w_time_hbm, w_up_hbm, _w_time, _w_up, _taps,
-    out_ref, w_time_ref, w_up_ref, taps_ref, wide_ref, done_ref, sems, *, rows, width,
+    own_ref, w_in_ref, b_in_ref, gain_ref, b_time_ref, b_up_ref, w_up_ref, w_time_hbm, _w_time,
+    out_ref, w_time_ref, taps_ref, wide_ref, done_ref, sems, *, rows, width,
 ):
     time = lax.axis_index("tm")
 
     @pl.when(time == 0)
     def _():
+        prepare_taps(w_up_ref, taps_ref)
         own = own_ref[...]
         hidden = entry(jnp.concatenate([jnp.zeros_like(own), own], axis=0), w_in_ref, b_in_ref, rows, width)
         timed = own_part(normalized(hidden, gain_ref), w_time_ref) + b_time_ref[...][None, :]
@@ -227,51 +214,34 @@
 
     @pl.when(time > 1)
     def _():
-        time_copy, up_copy = copies_of((w_time_hbm, w_up_hbm), (w_time_ref, w_up_ref), sems)
-        up_copy.start()
-        time_copy.start()
-        up_copy.wait()
+        copy = pltpu.make_async_copy(w_time_hbm, w_time_ref, sems.at[0])
+        copy.start()
         prepare_taps(w_up_ref, taps_ref)
-        time_copy.wait()
+        copy.wait()
 
     @pl.when(time == 1)
     def _():
         prepare_taps(w_up_ref, taps_ref)
 
 
-def middle_kernel(
+def second_kernel(
     own_ref, one_ref, w_in_ref, b_in_ref, gain_ref, b_time_ref, b_up_ref, w_time_ref, taps_ref, _out,
-    out_ref, hidden_ref, timed_ref, wide_ref, done_ref, sems, *, rows, width,
+    out_ref, *scratch, rows, width,
 ):
-    time = lax.axis_index("tm")
-    size = hidden_ref.shape[0]
-
-    def known():
+    @pl.when(lax.axis_index("tm") == 1)
+    def _():
         frames = jnp.concatenate([jnp.zeros_like(one_ref), one_ref[...], own_ref[...]], axis=0)
-        return entry(frames, w_in_ref, b_in_ref, rows, width)
-
-    @pl.when(time == 1)
-    def _():
-        active = normalized(known(), gain_ref)
-        timed = own_part(active[size:], w_time_ref) + earlier_part(active[:size], w_time_ref) + b_time_ref[...][None, :]
-        upsample(timed, taps_ref, b_up_ref, out_ref, wide_ref, done_ref, sems, rows, own_ref.shape[1])
-
-    @pl.when(time > 1)
-    def _():
-        hidden = known()
-        hidden_ref[...] = hidden[:size]
-        timed_ref[...] = own_part(normalized(hidden[size:], gain_ref), w_time_ref) + b_time_ref[...][None, :]
+        finish(frames, w_in_ref, b_in_ref, gain_ref, b_time_ref, b_up_ref, w_time_ref, taps_ref, out_ref, scratch, rows, width)
 
 
 def last_kernel(
-    two_ref, hidden_ref, timed_ref, w_in_ref, gain_ref, b_up_ref, w_time_ref, taps_ref, _out,
-    out_ref, wide_ref, done_ref, sems, *, rows, width,
+    own_ref, two_ref, one_ref, w_in_ref, b_in_ref, gain_ref, b_time_ref, b_up_ref, w_time_ref, taps_ref, _out,
+    out_ref, *scratch, rows, width,
 ):
     @pl.when(lax.axis_index("tm") > 1)
     def _():
-        active = normalized(hidden_ref[...] + entry_of_two(two_ref[...], w_in_ref, rows, width), gain_ref)
-        timed = timed_ref[...] + earlier_part(active, w_time_ref)
-        upsample(timed, taps_ref, b_up_ref, out_ref, wide_ref, done_ref, sems, rows, two_ref.shape[1])
+        frames = jnp.concatenate([two_ref[...], one_ref[...], own_ref[...]], axis=0)
+        finish(frames, w_in_ref, b_in_ref, gain_ref, b_time_ref, b_up_ref, w_time_ref, taps_ref, out_ref, scratch, rows, width)
 
 
 def params(mib):
@@ -288,8 +258,8 @@
 
     even = swapped(latent, "space", 0)
     odd = swapped(latent, "space", 1)
-    arrays = [in_hbm(x) for x in (w_in.reshape(-1, features), b_in, gain_in, b_time, b_up, latent)] + [w_time, w_up]
-    w_in, b_in, gain_in, b_time, b_up, own, w_time_kept, w_up_kept = pl.pallas_call(
+    arrays = [in_hbm(x) for x in (w_in.reshape(-1, features), b_in, gain_in, b_time, b_up, latent)] + [w_up, w_time]
+    w_in, b_in, gain_in, b_time, b_up, own, w_up, w_time_kept = pl.pallas_call(
         stage_kernel,
         out_shape=[pltpu.VMEM(x.shape, x.dtype) for x in arrays],
         in_specs=[HBM] * len(arrays),
@@ -297,52 +267,52 @@
         scratch_shapes=[pltpu.SemaphoreType.DMA((len(arrays),))],
         compiler_params=params(1),
     )(*arrays)
-    positions = frames * (rows + 2) * cols
-    timed_shape = pltpu.VMEM((positions, 2 * features), jnp.float32)
     taps_shape = pltpu.VMEM((2, 3, 2 * features, out_width), jnp.bfloat16)
-    own, taps = pl.pallas_call(
+    own = pl.pallas_call(
         pack_kernel,
-        out_shape=[pltpu.VMEM((frames, cols, LANES), latent.dtype), taps_shape],
-        in_specs=[VMEM] * 4,
-        out_specs=[VMEM] * 2,
-        compiler_params=params(4),
-    )(odd, even, own, w_up_kept)
-    one = shifted(own, "tm", 1)
-    two = shifted(own, "tm", 2)
-
-    finish = [
+        out_shape=pltpu.VMEM((frames, cols, LANES), latent.dtype),
+        in_specs=[VMEM] * 3,
+        out_specs=VMEM,
+        compiler_params=params(1),
+    )(odd, even, own)
+    times = lax.axis_size("tm")
+    first = moved(own, lambda t: (1 - t) % times if t < 2 else t)
+    two = moved(own, lambda t: (t + 2) % times)
+    one = moved(own, lambda t: t if t == 0 else t % (times - 1) + 1)
+
+    scratch = [
         pltpu.VMEM((2, 2, 2 * frames * rows * 2 * cols, LANES), jnp.float32),
         pltpu.VMEM((2, 2 * frames, rows, 2 * cols, out_width), jnp.bfloat16),
         pltpu.SemaphoreType.DMA((2,)),
     ]
     result = pltpu.HBM(out_shape, jnp.bfloat16)
-    out, w_time_kept, w_up_kept, taps = pl.pallas_call(
+    out, w_time_kept, taps = pl.pallas_call(
         functools.partial(first_kernel, rows=rows, width=width),
-        out_shape=[result] + [pltpu.VMEM(w.shape, w.dtype) for w in (w_time, w_up)] + [taps_shape],
-        in_specs=[VMEM] * 6 + [HBM] * 2 + [VMEM] * 3,
-        out_specs=[HBM] + [VMEM] * 3,
-        scratch_shapes=finish,
-        input_output_aliases={8: 1, 9: 2, 10: 3},
+        out_shape=[result, pltpu.VMEM(w_time.shape, w_time.dtype), taps_shape],
+        in_specs=[VMEM] * 7 + [HBM, VMEM],
+        out_specs=[HBM] + [VMEM] * 2,
+        scratch_shapes=scratch,
+        input_output_aliases={8: 1},
         compiler_params=params(16),
-    )(own, w_in, b_in, gain_in, b_time, b_up, w_time, w_up, w_time_kept, w_up_kept, taps)
-    out, hidden, timed = pl.pallas_call(
-        functools.partial(middle_kernel, rows=rows, width=width),
-        out_shape=[result, pltpu.VMEM((positions, features), jnp.float32), timed_shape],
+    )(own, w_in, b_in, gain_in, b_time, b_up, w_up, w_time, w_time_kept)
+    out = pl.pallas_call(
+        functools.partial(second_kernel, rows=rows, width=width),
+        out_shape=result,
         in_specs=[VMEM] * 9 + [HBM],
-        out_specs=[HBM, VMEM, VMEM],
-        scratch_shapes=finish,
+        out_specs=HBM,
+        scratch_shapes=scratch,
         input_output_aliases={9: 0},
         compiler_params=params(16),
-    )(own, one, w_in, b_in, gain_in, b_time, b_up, w_time_kept, taps, out)
+    )(own, first, w_in, b_in, gain_in, b_time, b_up, w_time_kept, taps, out)
     out = pl.pallas_call(
         functools.partial(last_kernel, rows=rows, width=width),
-        out_shape=pltpu.HBM(out_shape, jnp.bfloat16),
-        in_specs=[VMEM] * 8 + [HBM],
+        out_shape=result,
+        in_specs=[VMEM] * 10 + [HBM],
         out_specs=HBM,
-        scratch_shapes=finish,
-        input_output_aliases={8: 0},
+        scratch_shapes=scratch,
+        input_output_aliases={10: 0},
         compiler_params=params(16),
-    )(two, hidden, timed, w_in, gain_in, b_up, w_time_kept, taps, out)
+    )(own, two, one, w_in, b_in, gain_in, b_time, b_up, w_time_kept, taps, out)
     return out.reshape(2 * frames, 2 * rows, 2 * cols, out_width)
 
 

time: 11.8 us -> 11.2 us (0.949)
  the two profiles are of different devices: /device:TPU:18 before, /device:TPU:20 now
where the time goes in v4:
time: 11.2 us; the launch traced here: 11 us
  Pallas kernels  5.48 us (49%)
  starting transfers between devices  3.94 us (35%)
  waiting for transfers between devices  1.55 us (14%)
    ppermute x3, starting transfers between devices, moved(): return lax.ppermute(x, ('tm', 'space'), pairs)  2.33 us
    pallas_call x1, Pallas kernels, shards(): pl.pallas_call(functools.partial(last_kernel, rows=rows, width=width), ou...  2.23 us
    ppermute x2, starting transfers between devices, swapped(): return lax.ppermute(x, axis, pairs)  1.61 us
    pallas_call x1, Pallas kernels, shards(): pl.pallas_call(stage_kernel, out_shape=[pltpu.VMEM(x.shape, x.dtype) for...  1.58 us
    pallas_call x1, Pallas kernels, shards(): pl.pallas_call(functools.partial(first_kernel, rows=rows, width=width), o...  1.5 us
    ppermute x3, waiting for transfers between devices, moved(): return lax.ppermute(x, ('tm', 'space'), pairs)  1.24 us
    ppermute x2, waiting for transfers between devices, swapped(): return lax.ppermute(x, axis, pairs)  0.31 us
  transfers between devices with their start and end apart: 5, of which 3 were waited for; matrix products, arithmetic and copies ran while one was open for 0% of the time, Pallas kernels for 28%

profile of v4, /device:TPU:20, one launch (start us, length us, event | category | flops | bytes accessed | tf_op | source)
XLA Modules:
  0.0 11.0 jit_solution(1169897525663998698)
XLA Ops:
  0.0 0.9 %collective-permute-start = (bf16[2,2,16,16]{3,2,1,0:T(8,128)(2,1)}, bf16[2,2,16,16]{3,2,1,0:T(8,128)(2,1)S(1)}, u32[]{:S(2)}, u32[]{:S(2)}) collective-permute-start(bf16[2,2,16,16]{3,2,1,0:T(8,128)(2,1)} %refs_5_.1), channel_id=1, source_target_pairs={{1,2},{2,1},{3,0},{0,3},{5,6},{6,5},{7,4},{4,7},{9,10},{10,9},{11,... | collective-permute-start | bytes 6152 | tf_op jit(solution)/shard_map/ppermute | solution.py:22
  0.9 0.7 %collective-permute-start.1 = (bf16[2,2,16,16]{3,2,1,0:T(8,128)(2,1)}, bf16[2,2,16,16]{3,2,1,0:T(8,128)(2,1)S(1)}, u32[]{:S(2)}, u32[]{:S(2)}) collective-permute-start(bf16[2,2,16,16]{3,2,1,0:T(8,128)(2,1)} %refs_5_.1), channel_id=1, source_target_pairs={{0,1},{1,0},{2,3},{3,2},{4,5},{5,4},{6,7},{7,6},{8,9},{9,8},{10,11... | collective-permute-start | bytes 6152 | tf_op jit(solution)/shard_map/ppermute | solution.py:22
  1.6 1.6 %shard_map.82 = (bf16[432,384]{1,0:T(8,128)(2,1)S(1)}, f32[384]{0:T(512)S(1)}, f32[384]{0:T(512)S(1)}, f32[768]{0:T(1024)S(1)}, f32[192]{0:T(256)S(1)}, /*index=...) custom-call(bf16[432,384]{1,0:T(8,128)(2,1)} %bitcast.9, f32[384]{0:T(512)} %refs_1_.1, ...), custom_call_target="tpu_custom_call" | custom-call | tf_op jit(solution)/shard_map/pallas_call | solution.py:262
  3.2 0.3 %collective-permute-done.odd_ref = bf16[2,2,16,16]{3,2,1,0:T(8,128)(2,1)S(1)} collective-permute-done((bf16[2,2,16,16]{3,2,1,0:T(8,128)(2,1)}, bf16[2,2,16,16]{3,2,1,0:T(8,128)(2,1)S(1)}, u32[]{:S(2)}, u32[]{:S(2)}) %collective-permute-start) | collective-permute-done | bytes 2080 | tf_op jit(solution)/shard_map/ppermute | solution.py:22
  3.5 0.0 collective-permute-done.1.even_ref
  3.5 0.1 %shard_map.83.own_ref = bf16[2,16,128]{2,1,0:T(8,128)(2,1)S(1)} custom-call(bf16[2,2,16,16]{3,2,1,0:T(8,128)(2,1)S(1)} %collective-permute-done.odd_ref, bf16[2,2,16,16]{3,2,1,0:T(8,128)(2,1)S(1)} %collective-permute-done.1.even_ref, bf16[2,2,16,16]{3,2,1,0:T(8,128)(2,1)S(1)} %get-tuple-element.16.own_ref), custom_call_target="tpu_custom_call" | custom-call | tf_op jit(solution)/shard_map/pallas_call | solution.py:271
  3.6 0.1 %collective-permute-start.4 = (bf16[2,16,128]{2,1,0:T(8,128)(2,1)S(1)}, bf16[2,16,128]{2,1,0:T(8,128)(2,1)S(1)}, u32[]{:S(2)}, u32[]{:S(2)}) collective-permute-start(bf16[2,16,128]{2,1,0:T(8,128)(2,1)S(1)} %shard_map.83.own_ref), channel_id=1, source_target_pairs={{0,4},{1,5},{2,6},{3,7},{4,1},{5,0},{6,3},{7,2},{8,9},{9,8},{10,11... | collective-permute-start | bytes 24584 | tf_op jit(solution)/shard_map/ppermute | solution.py:32
  3.8 1.4 %collective-permute-start.2 = (bf16[2,16,128]{2,1,0:T(8,128)(2,1)S(1)}, bf16[2,16,128]{2,1,0:T(8,128)(2,1)S(1)}, u32[]{:S(2)}, u32[]{:S(2)}) collective-permute-start(bf16[2,16,128]{2,1,0:T(8,128)(2,1)S(1)} %shard_map.83.own_ref), channel_id=1, source_target_pairs={{0,8},{1,9},{2,10},{3,11},{4,12},{5,13},{6,14},{7,15},{8,1},{9,0},... | collective-permute-start | bytes 24584 | tf_op jit(solution)/shard_map/ppermute | solution.py:32
  5.1 0.8 %collective-permute-start.3 = (bf16[2,16,128]{2,1,0:T(8,128)(2,1)S(1)}, bf16[2,16,128]{2,1,0:T(8,128)(2,1)S(1)}, u32[]{:S(2)}, u32[]{:S(2)}) collective-permute-start(bf16[2,16,128]{2,1,0:T(8,128)(2,1)S(1)} %shard_map.83.own_ref), channel_id=1, source_target_pairs={{0,1},{1,0},{2,3},{3,2},{4,8},{5,9},{6,10},{7,11},{8,12},{9,13},{1... | collective-permute-start | bytes 24584 | tf_op jit(solution)/shard_map/ppermute | solution.py:32
  6.0 1.5 %shard_map.84 = (bf16[4,2,2,32,192]{4,3,2,1,0:T(8,128)(2,1)}, bf16[1152,768]{1,0:T(8,128)(2,1)S(1)}, bf16[2,3,768,192]{3,2,1,0:T(8,128)(2,1)S(1)}) custom-call(bf16[2,16,128]{2,1,0:T(8,128)(2,1)S(1)} %shard_map.83.own_ref, bf16[432,384]{1,0:T(8,128)(2,1)S(1)} %get-tuple-element.17.w_in_ref, ...), custom_call_target="tpu_custom_call", output_to_operand_aliasing={{1}: (8, {})} | custom-call | tf_op jit(solution)/shard_map/pallas_call | solution.py:289
  7.5 0.0 collective-permute-done.4.one_ref
  7.5 0.8 %collective-permute-done.2.two_ref = bf16[2,16,128]{2,1,0:T(8,128)(2,1)S(1)} collective-permute-done((bf16[2,16,128]{2,1,0:T(8,128)(2,1)S(1)}, bf16[2,16,128]{2,1,0:T(8,128)(2,1)S(1)}, u32[]{:S(2)}, u32[]{:S(2)}) %collective-permute-start.2) | collective-permute-done | bytes 8224 | tf_op jit(solution)/shard_map/ppermute | solution.py:32
  8.4 0.4 %collective-permute-done.3.one_ref = bf16[2,16,128]{2,1,0:T(8,128)(2,1)S(1)} collective-permute-done((bf16[2,16,128]{2,1,0:T(8,128)(2,1)S(1)}, bf16[2,16,128]{2,1,0:T(8,128)(2,1)S(1)}, u32[]{:S(2)}, u32[]{:S(2)}) %collective-permute-start.3) | collective-permute-done | bytes 8224 | tf_op jit(solution)/shard_map/ppermute | solution.py:32
  8.8 2.2 %shard_map.86 = bf16[4,2,2,32,192]{4,3,2,1,0:T(8,128)(2,1)} custom-call(bf16[2,16,128]{2,1,0:T(8,128)(2,1)S(1)} %shard_map.83.own_ref, bf16[2,16,128]{2,1,0:T(8,128)(2,1)S(1)} %collective-permute-done.2.two_ref, bf16[2,16,128]{2,1,0:T(8,128)(2,1)S(1)} %collective-permute-done.3.one_ref, ...), custom_call_target="tpu_custom_call", output_to_operand_aliasing={{}: (10, {})} | custom-call | tf_op jit(solution)/shard_map/pallas_call | solution.py:307
  (1 shorter events, 0.0 us)
Async XLA Ops:
  0.0 3.5 %collective-permute-start = (bf16[2,2,16,16]{3,2,1,0:T(8,128)(2,1)}, bf16[2,2,16,16]{3,2,1,0:T(8,128)(2,1)S(1)}, u32[]{:S(2)}, u32[]{:S(2)}) collective-permute-start(bf16[2,2,16,16]{3,2,1,0:T(8,128)(2,1)} %refs_5_.1), channel_id=1, source_target_pairs={{1,2},{2,1},{3,0},{0,3},{5,6},{6,5},{7,4},{4,7},{9,10},{10,9},{11,... | collective-permute-start | bytes 6152 | tf_op jit(solution)/shard_map/ppermute | solution.py:22
  0.9 2.6 %collective-permute-start.1 = (bf16[2,2,16,16]{3,2,1,0:T(8,128)(2,1)}, bf16[2,2,16,16]{3,2,1,0:T(8,128)(2,1)S(1)}, u32[]{:S(2)}, u32[]{:S(2)}) collective-permute-start(bf16[2,2,16,16]{3,2,1,0:T(8,128)(2,1)} %refs_5_.1), channel_id=1, source_target_pairs={{0,1},{1,0},{2,3},{3,2},{4,5},{5,4},{6,7},{7,6},{8,9},{9,8},{10,11... | collective-permute-start | bytes 6152 | tf_op jit(solution)/shard_map/ppermute | solution.py:22
  3.6 3.8 %collective-permute-start.4 = (bf16[2,16,128]{2,1,0:T(8,128)(2,1)S(1)}, bf16[2,16,128]{2,1,0:T(8,128)(2,1)S(1)}, u32[]{:S(2)}, u32[]{:S(2)}) collective-permute-start(bf16[2,16,128]{2,1,0:T(8,128)(2,1)S(1)} %shard_map.83.own_ref), channel_id=1, source_target_pairs={{0,4},{1,5},{2,6},{3,7},{4,1},{5,0},{6,3},{7,2},{8,9},{9,8},{10,11... | collective-permute-start | bytes 24584 | tf_op jit(solution)/shard_map/ppermute | solution.py:32
  3.8 4.6 %collective-permute-start.2 = (bf16[2,16,128]{2,1,0:T(8,128)(2,1)S(1)}, bf16[2,16,128]{2,1,0:T(8,128)(2,1)S(1)}, u32[]{:S(2)}, u32[]{:S(2)}) collective-permute-start(bf16[2,16,128]{2,1,0:T(8,128)(2,1)S(1)} %shard_map.83.own_ref), channel_id=1, source_target_pairs={{0,8},{1,9},{2,10},{3,11},{4,12},{5,13},{6,14},{7,15},{8,1},{9,0},... | collective-permute-start | bytes 24584 | tf_op jit(solution)/shard_map/ppermute | solution.py:32
  5.1 3.7 %collective-permute-start.3 = (bf16[2,16,128]{2,1,0:T(8,128)(2,1)S(1)}, bf16[2,16,128]{2,1,0:T(8,128)(2,1)S(1)}, u32[]{:S(2)}, u32[]{:S(2)}) collective-permute-start(bf16[2,16,128]{2,1,0:T(8,128)(2,1)S(1)} %shard_map.83.own_ref), channel_id=1, source_target_pairs={{0,1},{1,0},{2,3},{3,2},{4,8},{5,9},{6,10},{7,11},{8,12},{9,13},{1... | collective-permute-start | bytes 24584 | tf_op jit(solution)/shard_map/ppermute | solution.py:32

commit v5 on v4

--- a/solution.py
+++ b/solution.py
@@ -43,20 +43,10 @@
 def stage_kernel(*refs):
     count = len(refs) // 2
     copies = copies_of(refs[:count], refs[count:-1], refs[-1])
-    early = lax.axis_index("tm") <= 1
-
-    @pl.when(early)
-    def _():
-        copies[-1].start()
-
-    for copy in copies[:-1]:
+    for copy in copies:
         copy.start()
-    for copy in copies[:-1]:
+    for copy in copies:
         copy.wait()
-
-    @pl.when(early)
-    def _():
-        copies[-1].wait()
 
 
 def pack_kernel(odd_ref, even_ref, own_ref, packed_ref):
@@ -127,23 +117,20 @@
     return (half + half * jnp.tanh(half)).astype(jnp.bfloat16)
 
 
-def own_part(active, w_time_ref):
-    features = active.shape[1]
-    block = active.shape[0] // 2
-    early, late = active[:block], active[block:]
-    left = jnp.concatenate(
-        [jnp.concatenate([jnp.zeros_like(early), early], axis=1), jnp.concatenate([early, late], axis=1)], axis=0
-    )
-    return jnp.dot(left, w_time_ref[features:, :], preferred_element_type=jnp.float32)
-
-
 def finish(frames, w_in_ref, b_in_ref, gain_ref, b_time_ref, b_up_ref, w_time_ref, taps_ref, out_ref, scratch, rows, width):
     cols = frames.shape[1]
+    features = w_in_ref.shape[1]
     active = normalized(entry(frames, w_in_ref, b_in_ref, rows, width), gain_ref)
     block = (rows + 2) * cols
-    left = jnp.concatenate([active[a * block : (a + 2) * block] for a in range(3)], axis=1)
-    timed = jnp.dot(left, w_time_ref[...], preferred_element_type=jnp.float32) + b_time_ref[...][None, :]
-    upsample(timed, taps_ref, b_up_ref, out_ref, *scratch, rows, cols)
+    if frames.shape[0] == 4:
+        early, late = active[:block], active[block:]
+        left = [jnp.concatenate([jnp.zeros_like(early), early], axis=0), active]
+        w_time = w_time_ref[features:, :]
+    else:
+        left = [active[a * block : (a + 2) * block] for a in range(3)]
+        w_time = w_time_ref[...]
+    timed = jnp.dot(jnp.concatenate(left, axis=1), w_time, preferred_element_type=jnp.float32)
+    upsample(timed + b_time_ref[...][None, :], taps_ref, b_up_ref, out_ref, *scratch, rows, cols)
 
 
 def prepare_taps(w_up_ref, taps_ref):
@@ -199,27 +186,17 @@
 
 
 def first_kernel(
-    own_ref, w_in_ref, b_in_ref, gain_ref, b_time_ref, b_up_ref, w_up_ref, w_time_hbm, _w_time,
-    out_ref, w_time_ref, taps_ref, wide_ref, done_ref, sems, *, rows, width,
+    own_ref, w_in_ref, b_in_ref, gain_ref, b_time_ref, b_up_ref, w_time_ref, w_up_ref, out_ref, taps_ref, *scratch, rows, width
 ):
     time = lax.axis_index("tm")
 
     @pl.when(time == 0)
     def _():
         prepare_taps(w_up_ref, taps_ref)
-        own = own_ref[...]
-        hidden = entry(jnp.concatenate([jnp.zeros_like(own), own], axis=0), w_in_ref, b_in_ref, rows, width)
-        timed = own_part(normalized(hidden, gain_ref), w_time_ref) + b_time_ref[...][None, :]
-        upsample(timed, taps_ref, b_up_ref, out_ref, wide_ref, done_ref, sems, rows, own.shape[1])
-
-    @pl.when(time > 1)
-    def _():
-        copy = pltpu.make_async_copy(w_time_hbm, w_time_ref, sems.at[0])
-        copy.start()
-        prepare_taps(w_up_ref, taps_ref)
-        copy.wait()
-
-    @pl.when(time == 1)
+        frames = jnp.concatenate([jnp.zeros_like(own_ref), own_ref[...]], axis=0)
+        finish(frames, w_in_ref, b_in_ref, gain_ref, b_time_ref, b_up_ref, w_time_ref, taps_ref, out_ref, scratch, rows, width)
+
+    @pl.when(time > 0)
     def _():
         prepare_taps(w_up_ref, taps_ref)
 
@@ -258,8 +235,8 @@
 
     even = swapped(latent, "space", 0)
     odd = swapped(latent, "space", 1)
-    arrays = [in_hbm(x) for x in (w_in.reshape(-1, features), b_in, gain_in, b_time, b_up, latent)] + [w_up, w_time]
-    w_in, b_in, gain_in, b_time, b_up, own, w_up, w_time_kept = pl.pallas_call(
+    arrays = [w_time, w_up] + [in_hbm(x) for x in (w_in.reshape(-1, features), b_in, gain_in, b_time, b_up, latent)]
+    w_time, w_up, w_in, b_in, gain_in, b_time, b_up, own = pl.pallas_call(
         stage_kernel,
         out_shape=[pltpu.VMEM(x.shape, x.dtype) for x in arrays],
         in_specs=[HBM] * len(arrays),
@@ -267,7 +244,6 @@
         scratch_shapes=[pltpu.SemaphoreType.DMA((len(arrays),))],
         compiler_params=params(1),
     )(*arrays)
-    taps_shape = pltpu.VMEM((2, 3, 2 * features, out_width), jnp.bfloat16)
     own = pl.pallas_call(
         pack_kernel,
         out_shape=pltpu.VMEM((frames, cols, LANES), latent.dtype),
@@ -286,15 +262,14 @@
         pltpu.SemaphoreType.DMA((2,)),
     ]
     result = pltpu.HBM(out_shape, jnp.bfloat16)
-    out, w_time_kept, taps = pl.pallas_call(
+    out, taps = pl.pallas_call(
         functools.partial(first_kernel, rows=rows, width=width),
-        out_shape=[result, pltpu.VMEM(w_time.shape, w_time.dtype), taps_shape],
-        in_specs=[VMEM] * 7 + [HBM, VMEM],
-        out_specs=[HBM] + [VMEM] * 2,
+        out_shape=[result, pltpu.VMEM((2, 3, 2 * features, out_width), jnp.bfloat16)],
+        in_specs=[VMEM] * 8,
+        out_specs=[HBM, VMEM],
         scratch_shapes=scratch,
-        input_output_aliases={8: 1},
         compiler_params=params(16),
-    )(own, w_in, b_in, gain_in, b_time, b_up, w_up, w_time, w_time_kept)
+    )(own, w_in, b_in, gain_in, b_time, b_up, w_time, w_up)
     out = pl.pallas_call(
         functools.partial(second_kernel, rows=rows, width=width),
         out_shape=result,
@@ -303,7 +278,7 @@
         scratch_shapes=scratch,
         input_output_aliases={9: 0},
         compiler_params=params(16),
-    )(own, first, w_in, b_in, gain_in, b_time, b_up, w_time_kept, taps, out)
+    )(own, first, w_in, b_in, gain_in, b_time, b_up, w_time, taps, out)
     out = pl.pallas_call(
         functools.partial(last_kernel, rows=rows, width=width),
         out_shape=result,
@@ -312,7 +287,7 @@
         scratch_shapes=scratch,
         input_output_aliases={10: 0},
         compiler_params=params(16),
-    )(own, two, one, w_in, b_in, gain_in, b_time, b_up, w_time_kept, taps, out)
+    )(own, two, one, w_in, b_in, gain_in, b_time, b_up, w_time, taps, out)
     return out.reshape(2 * frames, 2 * rows, 2 * cols, out_width)
 
 

time: 11.2 us -> 11.1 us (level)
  the two profiles are of different devices: /device:TPU:20 before, /device:TPU:18 now
where the time goes in v5:
time: 11.1 us; the launch traced here: 10.9 us
  Pallas kernels  5 us (45%)
  waiting for transfers between devices  3.09 us (28%)
  starting transfers between devices  2.79 us (25%)
    pallas_call x1, Pallas kernels, shards(): pl.pallas_call(functools.partial(last_kernel, rows=rows, width=width), ou...  2.23 us
    ppermute x3, waiting for transfers between devices, moved(): return lax.ppermute(x, ('tm', 'space'), pairs)  2.2 us
    ppermute x3, starting transfers between devices, moved(): return lax.ppermute(x, ('tm', 'space'), pairs)  2.14 us
    pallas_call x1, Pallas kernels, shards(): pl.pallas_call(stage_kernel, out_shape=[pltpu.VMEM(x.shape, x.dtype) for...  1.98 us
    ppermute x2, waiting for transfers between devices, swapped(): return lax.ppermute(x, axis, pairs)  0.89 us
    ppermute x2, starting transfers between devices, swapped(): return lax.ppermute(x, axis, pairs)  0.65 us
    pallas_call x1, Pallas kernels, shards(): pl.pallas_call(functools.partial(first_kernel, rows=rows, width=width), o...  0.62 us
  transfers between devices with their start and end apart: 5, of which 3 were waited for; matrix products, arithmetic and copies ran while one was open for 0% of the time, Pallas kernels for 24%

profile of v5, /device:TPU:18, one launch (start us, length us, event | category | flops | bytes accessed | tf_op | source)
XLA Modules:
  0.0 10.9 jit_solution(835597165555660759)
XLA Ops:
  0.0 0.0 collective-permute-start
  0.0 0.6 %collective-permute-start.1 = (bf16[2,2,16,16]{3,2,1,0:T(8,128)(2,1)}, bf16[2,2,16,16]{3,2,1,0:T(8,128)(2,1)S(1)}, u32[]{:S(2)}, u32[]{:S(2)}) collective-permute-start(bf16[2,2,16,16]{3,2,1,0:T(8,128)(2,1)} %refs_7_.1), channel_id=1, source_target_pairs={{0,1},{1,0},{2,3},{3,2},{4,5},{5,4},{6,7},{7,6},{8,9},{9,8},{10,11... | collective-permute-start | bytes 6152 | tf_op jit(solution)/shard_map/ppermute | solution.py:22
  0.7 2.0 %shard_map.82 = (bf16[1152,768]{1,0:T(8,128)(2,1)S(1)}, bf16[1728,384]{1,0:T(8,128)(2,1)S(1)}, bf16[432,384]{1,0:T(8,128)(2,1)S(1)}, f32[384]{0:T(512)S(1)}, f32...) custom-call(bf16[1152,768]{1,0:T(8,128)(2,1)} %bitcast.6, ...), custom_call_target="tpu_custom_call" | custom-call | tf_op jit(solution)/shard_map/pallas_call | solution.py:239
  2.6 0.9 %collective-permute-done.odd_ref = bf16[2,2,16,16]{3,2,1,0:T(8,128)(2,1)S(1)} collective-permute-done((bf16[2,2,16,16]{3,2,1,0:T(8,128)(2,1)}, bf16[2,2,16,16]{3,2,1,0:T(8,128)(2,1)S(1)}, u32[]{:S(2)}, u32[]{:S(2)}) %collective-permute-start) | collective-permute-done | bytes 2080 | tf_op jit(solution)/shard_map/ppermute | solution.py:22
  3.5 0.0 collective-permute-done.1.even_ref
  3.5 0.1 %shard_map.83.own_ref = bf16[2,16,128]{2,1,0:T(8,128)(2,1)S(1)} custom-call(bf16[2,2,16,16]{3,2,1,0:T(8,128)(2,1)S(1)} %collective-permute-done.odd_ref, bf16[2,2,16,16]{3,2,1,0:T(8,128)(2,1)S(1)} %collective-permute-done.1.even_ref, bf16[2,2,16,16]{3,2,1,0:T(8,128)(2,1)S(1)} %get-tuple-element.15.own_ref), custom_call_target="tpu_custom_call" | custom-call | tf_op jit(solution)/shard_map/pallas_call | solution.py:247
  3.7 0.1 %collective-permute-start.4 = (bf16[2,16,128]{2,1,0:T(8,128)(2,1)S(1)}, bf16[2,16,128]{2,1,0:T(8,128)(2,1)S(1)}, u32[]{:S(2)}, u32[]{:S(2)}) collective-permute-start(bf16[2,16,128]{2,1,0:T(8,128)(2,1)S(1)} %shard_map.83.own_ref), channel_id=1, source_target_pairs={{0,4},{1,5},{2,6},{3,7},{4,1},{5,0},{6,3},{7,2},{8,9},{9,8},{10,11... | collective-permute-start | bytes 24584 | tf_op jit(solution)/shard_map/ppermute | solution.py:32
  3.8 1.2 %collective-permute-start.2 = (bf16[2,16,128]{2,1,0:T(8,128)(2,1)S(1)}, bf16[2,16,128]{2,1,0:T(8,128)(2,1)S(1)}, u32[]{:S(2)}, u32[]{:S(2)}) collective-permute-start(bf16[2,16,128]{2,1,0:T(8,128)(2,1)S(1)} %shard_map.83.own_ref), channel_id=1, source_target_pairs={{0,8},{1,9},{2,10},{3,11},{4,12},{5,13},{6,14},{7,15},{8,1},{9,0},... | collective-permute-start | bytes 24584 | tf_op jit(solution)/shard_map/ppermute | solution.py:32
  5.0 0.8 %collective-permute-start.3 = (bf16[2,16,128]{2,1,0:T(8,128)(2,1)S(1)}, bf16[2,16,128]{2,1,0:T(8,128)(2,1)S(1)}, u32[]{:S(2)}, u32[]{:S(2)}) collective-permute-start(bf16[2,16,128]{2,1,0:T(8,128)(2,1)S(1)} %shard_map.83.own_ref), channel_id=1, source_target_pairs={{0,1},{1,0},{2,3},{3,2},{4,8},{5,9},{6,10},{7,11},{8,12},{9,13},{1... | collective-permute-start | bytes 24584 | tf_op jit(solution)/shard_map/ppermute | solution.py:32
  5.8 0.6 %shard_map.84 = (bf16[4,2,2,32,192]{4,3,2,1,0:T(8,128)(2,1)}, bf16[2,3,768,192]{3,2,1,0:T(8,128)(2,1)S(1)}) custom-call(bf16[2,16,128]{2,1,0:T(8,128)(2,1)S(1)} %shard_map.83.own_ref, bf16[432,384]{1,0:T(8,128)(2,1)S(1)} %get-tuple-element.16.w_in_ref, f32[384]{0:T(512)S(1)} %get-tuple-element.17.b_in_ref, f32[384]{0:T(512)S(1)} %get-tuple-element.18.gain_ref, ...), custom_call_target="tpu_custom_call" | custom-call | tf_op jit(solution)/shard_map/pallas_call | solution.py:265
  6.4 0.0 collective-permute-done.4.one_ref
  6.5 1.9 %collective-permute-done.2.two_ref = bf16[2,16,128]{2,1,0:T(8,128)(2,1)S(1)} collective-permute-done((bf16[2,16,128]{2,1,0:T(8,128)(2,1)S(1)}, bf16[2,16,128]{2,1,0:T(8,128)(2,1)S(1)}, u32[]{:S(2)}, u32[]{:S(2)}) %collective-permute-start.2) | collective-permute-done | bytes 8224 | tf_op jit(solution)/shard_map/ppermute | solution.py:32
  8.4 0.3 %collective-permute-done.3.one_ref = bf16[2,16,128]{2,1,0:T(8,128)(2,1)S(1)} collective-permute-done((bf16[2,16,128]{2,1,0:T(8,128)(2,1)S(1)}, bf16[2,16,128]{2,1,0:T(8,128)(2,1)S(1)}, u32[]{:S(2)}, u32[]{:S(2)}) %collective-permute-start.3) | collective-permute-done | bytes 8224 | tf_op jit(solution)/shard_map/ppermute | solution.py:32
  8.7 2.2 %shard_map.86 = bf16[4,2,2,32,192]{4,3,2,1,0:T(8,128)(2,1)} custom-call(bf16[2,16,128]{2,1,0:T(8,128)(2,1)S(1)} %shard_map.83.own_ref, bf16[2,16,128]{2,1,0:T(8,128)(2,1)S(1)} %collective-permute-done.2.two_ref, bf16[2,16,128]{2,1,0:T(8,128)(2,1)S(1)} %collective-permute-done.3.one_ref, ...), custom_call_target="tpu_custom_call", output_to_operand_aliasing={{}: (10, {})} | custom-call | tf_op jit(solution)/shard_map/pallas_call | solution.py:282
  (1 shorter events, 0.0 us)
Async XLA Ops:
  0.0 3.5 %collective-permute-start = (bf16[2,2,16,16]{3,2,1,0:T(8,128)(2,1)}, bf16[2,2,16,16]{3,2,1,0:T(8,128)(2,1)S(1)}, u32[]{:S(2)}, u32[]{:S(2)}) collective-permute-start(bf16[2,2,16,16]{3,2,1,0:T(8,128)(2,1)} %refs_7_.1), channel_id=1, source_target_pairs={{1,2},{2,1},{3,0},{0,3},{5,6},{6,5},{7,4},{4,7},{9,10},{10,9},{11,... | collective-permute-start | bytes 6152 | tf_op jit(solution)/shard_map/ppermute | solution.py:22
  0.0 3.5 %collective-permute-start.1 = (bf16[2,2,16,16]{3,2,1,0:T(8,128)(2,1)}, bf16[2,2,16,16]{3,2,1,0:T(8,128)(2,1)S(1)}, u32[]{:S(2)}, u32[]{:S(2)}) collective-permute-start(bf16[2,2,16,16]{3,2,1,0:T(8,128)(2,1)} %refs_7_.1), channel_id=1, source_target_pairs={{0,1},{1,0},{2,3},{3,2},{4,5},{5,4},{6,7},{7,6},{8,9},{9,8},{10,11... | collective-permute-start | bytes 6152 | tf_op jit(solution)/shard_map/ppermute | solution.py:22
  3.7 2.8 %collective-permute-start.4 = (bf16[2,16,128]{2,1,0:T(8,128)(2,1)S(1)}, bf16[2,16,128]{2,1,0:T(8,128)(2,1)S(1)}, u32[]{:S(2)}, u32[]{:S(2)}) collective-permute-start(bf16[2,16,128]{2,1,0:T(8,128)(2,1)S(1)} %shard_map.83.own_ref), channel_id=1, source_target_pairs={{0,4},{1,5},{2,6},{3,7},{4,1},{5,0},{6,3},{7,2},{8,9},{9,8},{10,11... | collective-permute-start | bytes 24584 | tf_op jit(solution)/shard_map/ppermute | solution.py:32
  3.8 4.6 %collective-permute-start.2 = (bf16[2,16,128]{2,1,0:T(8,128)(2,1)S(1)}, bf16[2,16,128]{2,1,0:T(8,128)(2,1)S(1)}, u32[]{:S(2)}, u32[]{:S(2)}) collective-permute-start(bf16[2,16,128]{2,1,0:T(8,128)(2,1)S(1)} %shard_map.83.own_ref), channel_id=1, source_target_pairs={{0,8},{1,9},{2,10},{3,11},{4,12},{5,13},{6,14},{7,15},{8,1},{9,0},... | collective-permute-start | bytes 24584 | tf_op jit(solution)/shard_map/ppermute | solution.py:32
  5.0 3.7 %collective-permute-start.3 = (bf16[2,16,128]{2,1,0:T(8,128)(2,1)S(1)}, bf16[2,16,128]{2,1,0:T(8,128)(2,1)S(1)}, u32[]{:S(2)}, u32[]{:S(2)}) collective-permute-start(bf16[2,16,128]{2,1,0:T(8,128)(2,1)S(1)} %shard_map.83.own_ref), channel_id=1, source_target_pairs={{0,1},{1,0},{2,3},{3,2},{4,8},{5,9},{6,10},{7,11},{8,12},{9,13},{1... | collective-permute-start | bytes 24584 | tf_op jit(solution)/shard_map/ppermute | solution.py:32

commit v6 on v5

--- a/solution.py
+++ b/solution.py
@@ -28,7 +28,7 @@
     for t in range(times):
         target = target_of(t)
         for s in range(spaces):
-            pairs.append((t * spaces + s, target * spaces + (s if target > t else s ^ 1)))
+            pairs.append((t * spaces + s, target * spaces + (s ^ 1 if target == t or t - target > 1 else s)))
     return lax.ppermute(x, ("tm", "space"), pairs)
 
 
@@ -211,13 +211,13 @@
         finish(frames, w_in_ref, b_in_ref, gain_ref, b_time_ref, b_up_ref, w_time_ref, taps_ref, out_ref, scratch, rows, width)
 
 
-def last_kernel(
-    own_ref, two_ref, one_ref, w_in_ref, b_in_ref, gain_ref, b_time_ref, b_up_ref, w_time_ref, taps_ref, _out,
-    out_ref, *scratch, rows, width,
+def third_kernel(
+    own_ref, near_ref, two_ref, w_in_ref, b_in_ref, gain_ref, b_time_ref, b_up_ref, w_time_ref, taps_ref, _out,
+    out_ref, *scratch, rows, width, mine,
 ):
-    @pl.when(lax.axis_index("tm") > 1)
-    def _():
-        frames = jnp.concatenate([two_ref[...], one_ref[...], own_ref[...]], axis=0)
+    @pl.when(mine(lax.axis_index("tm")))
+    def _():
+        frames = jnp.concatenate([two_ref[...], near_ref[...], own_ref[...]], axis=0)
         finish(frames, w_in_ref, b_in_ref, gain_ref, b_time_ref, b_up_ref, w_time_ref, taps_ref, out_ref, scratch, rows, width)
 
 
@@ -252,9 +252,9 @@
         compiler_params=params(1),
     )(odd, even, own)
     times = lax.axis_size("tm")
-    first = moved(own, lambda t: (1 - t) % times if t < 2 else t)
+    first = moved(own, lambda t: (t + 1) % min(3, times) if t < 3 else t)
     two = moved(own, lambda t: (t + 2) % times)
-    one = moved(own, lambda t: t if t == 0 else t % (times - 1) + 1)
+    one = moved(own, lambda t: t if t < 2 else (t - 1) % (times - 2) + 2)
 
     scratch = [
         pltpu.VMEM((2, 2, 2 * frames * rows * 2 * cols, LANES), jnp.float32),
@@ -279,15 +279,16 @@
         input_output_aliases={9: 0},
         compiler_params=params(16),
     )(own, first, w_in, b_in, gain_in, b_time, b_up, w_time, taps, out)
-    out = pl.pallas_call(
-        functools.partial(last_kernel, rows=rows, width=width),
-        out_shape=result,
-        in_specs=[VMEM] * 10 + [HBM],
-        out_specs=HBM,
-        scratch_shapes=scratch,
-        input_output_aliases={10: 0},
-        compiler_params=params(16),
-    )(own, two, one, w_in, b_in, gain_in, b_time, b_up, w_time, taps, out)
+    for near, mine in ((first, lambda time: time == 2), (one, lambda time: time > 2)):
+        out = pl.pallas_call(
+            functools.partial(third_kernel, rows=rows, width=width, mine=mine),
+            out_shape=result,
+            in_specs=[VMEM] * 10 + [HBM],
+            out_specs=HBM,
+            scratch_shapes=scratch,
+            input_output_aliases={10: 0},
+            compiler_params=params(16),
+        )(own, near, two, w_in, b_in, gain_in, b_time, b_up, w_time, taps, out)
     return out.reshape(2 * frames, 2 * rows, 2 * cols, out_width)
 
 

time: 11.1 us -> 11.1 us (level)
  the two profiles are of different devices: /device:TPU:18 before, /device:TPU:0 now
where the time goes in v6:
time: 11.1 us; the launch traced here: 10.8 us
  starting transfers between devices  5.86 us (53%)
  Pallas kernels  4.2 us (38%)
  waiting for transfers between devices  0.72 us (6%)
    ppermute x2, starting transfers between devices, swapped(): return lax.ppermute(x, axis, pairs)  3.05 us
    ppermute x3, starting transfers between devices, moved(): return lax.ppermute(x, ('tm', 'space'), pairs)  2.81 us
    pallas_call x1, Pallas kernels, shards(): pl.pallas_call(functools.partial(first_kernel, rows=rows, width=width), o...  1.98 us
    pallas_call x1, Pallas kernels, shards(): pl.pallas_call(stage_kernel, out_shape=[pltpu.VMEM(x.shape, x.dtype) for...  1.98 us
    ppermute x3, waiting for transfers between devices, moved(): return lax.ppermute(x, ('tm', 'space'), pairs)  0.72 us
  transfers between devices with their start and end apart: 5, of which 1 were waited for; matrix products, arithmetic and copies ran while one was open for 0% of the time, Pallas kernels for 37%

profile of v6, /device:TPU:0, one launch (start us, length us, event | category | flops | bytes accessed | tf_op | source)
XLA Modules:
  0.0 10.8 jit_solution(874043216416973271)
XLA Ops:
  0.0 2.4 %collective-permute-start = (bf16[2,2,16,16]{3,2,1,0:T(8,128)(2,1)}, bf16[2,2,16,16]{3,2,1,0:T(8,128)(2,1)S(1)}, u32[]{:S(2)}, u32[]{:S(2)}) collective-permute-start(bf16[2,2,16,16]{3,2,1,0:T(8,128)(2,1)} %refs_7_.1), channel_id=1, source_target_pairs={{1,2},{2,1},{3,0},{0,3},{5,6},{6,5},{7,4},{4,7},{9,10},{10,9},{11,... | collective-permute-start | bytes 6152 | tf_op jit(solution)/shard_map/ppermute | solution.py:22
  2.4 0.7 %collective-permute-start.1 = (bf16[2,2,16,16]{3,2,1,0:T(8,128)(2,1)}, bf16[2,2,16,16]{3,2,1,0:T(8,128)(2,1)S(1)}, u32[]{:S(2)}, u32[]{:S(2)}) collective-permute-start(bf16[2,2,16,16]{3,2,1,0:T(8,128)(2,1)} %refs_7_.1), channel_id=1, source_target_pairs={{0,1},{1,0},{2,3},{3,2},{4,5},{5,4},{6,7},{7,6},{8,9},{9,8},{10,11... | collective-permute-start | bytes 6152 | tf_op jit(solution)/shard_map/ppermute | solution.py:22
  3.1 2.0 %shard_map.82 = (bf16[1152,768]{1,0:T(8,128)(2,1)S(1)}, bf16[1728,384]{1,0:T(8,128)(2,1)S(1)}, bf16[432,384]{1,0:T(8,128)(2,1)S(1)}, f32[384]{0:T(512)S(1)}, f32...) custom-call(bf16[1152,768]{1,0:T(8,128)(2,1)} %bitcast.6, ...), custom_call_target="tpu_custom_call" | custom-call | tf_op jit(solution)/shard_map/pallas_call | solution.py:239
  5.0 0.0 collective-permute-done.odd_ref
  5.1 0.0 collective-permute-done.1.even_ref
  5.1 0.1 %shard_map.83.own_ref = bf16[2,16,128]{2,1,0:T(8,128)(2,1)S(1)} custom-call(bf16[2,2,16,16]{3,2,1,0:T(8,128)(2,1)S(1)} %collective-permute-done.odd_ref, bf16[2,2,16,16]{3,2,1,0:T(8,128)(2,1)S(1)} %collective-permute-done.1.even_ref, bf16[2,2,16,16]{3,2,1,0:T(8,128)(2,1)S(1)} %get-tuple-element.15.own_ref), custom_call_target="tpu_custom_call" | custom-call | tf_op jit(solution)/shard_map/pallas_call | solution.py:247
  5.2 1.6 %collective-permute-start.4 = (bf16[2,16,128]{2,1,0:T(8,128)(2,1)S(1)}, bf16[2,16,128]{2,1,0:T(8,128)(2,1)S(1)}, u32[]{:S(2)}, u32[]{:S(2)}) collective-permute-start(bf16[2,16,128]{2,1,0:T(8,128)(2,1)S(1)} %shard_map.83.own_ref), channel_id=1, source_target_pairs={{0,4},{1,5},{2,6},{3,7},{4,8},{5,9},{6,10},{7,11},{8,1},{9,0},{10,... | collective-permute-start | bytes 24584 | tf_op jit(solution)/shard_map/ppermute | solution.py:32
  6.8 1.1 %collective-permute-start.3 = (bf16[2,16,128]{2,1,0:T(8,128)(2,1)S(1)}, bf16[2,16,128]{2,1,0:T(8,128)(2,1)S(1)}, u32[]{:S(2)}, u32[]{:S(2)}) collective-permute-start(bf16[2,16,128]{2,1,0:T(8,128)(2,1)S(1)} %shard_map.83.own_ref), channel_id=1, source_target_pairs={{0,8},{1,9},{2,10},{3,11},{4,12},{5,13},{6,14},{7,15},{8,1},{9,0},... | collective-permute-start | bytes 24584 | tf_op jit(solution)/shard_map/ppermute | solution.py:32
  7.9 0.1 %collective-permute-start.2 = (bf16[2,16,128]{2,1,0:T(8,128)(2,1)S(1)}, bf16[2,16,128]{2,1,0:T(8,128)(2,1)S(1)}, u32[]{:S(2)}, u32[]{:S(2)}) collective-permute-start(bf16[2,16,128]{2,1,0:T(8,128)(2,1)S(1)} %shard_map.83.own_ref), channel_id=1, source_target_pairs={{0,1},{1,0},{2,3},{3,2},{4,5},{5,4},{6,7},{7,6},{8,12},{9,13},{10,... | collective-permute-start | bytes 24584 | tf_op jit(solution)/shard_map/ppermute | solution.py:32
  8.0 2.0 %shard_map.84 = (bf16[4,2,2,32,192]{4,3,2,1,0:T(8,128)(2,1)}, bf16[2,3,768,192]{3,2,1,0:T(8,128)(2,1)S(1)}) custom-call(bf16[2,16,128]{2,1,0:T(8,128)(2,1)S(1)} %shard_map.83.own_ref, bf16[432,384]{1,0:T(8,128)(2,1)S(1)} %get-tuple-element.16.w_in_ref, f32[384]{0:T(512)S(1)} %get-tuple-element.17.b_in_ref, f32[384]{0:T(512)S(1)} %get-tuple-element.18.gain_ref, ...), custom_call_target="tpu_custom_call" | custom-call | tf_op jit(solution)/shard_map/pallas_call | solution.py:265
  10.0 0.0 collective-permute-done.4.one_ref.near_ref
  10.1 0.7 %collective-permute-done.3.two_ref = bf16[2,16,128]{2,1,0:T(8,128)(2,1)S(1)} collective-permute-done((bf16[2,16,128]{2,1,0:T(8,128)(2,1)S(1)}, bf16[2,16,128]{2,1,0:T(8,128)(2,1)S(1)}, u32[]{:S(2)}, u32[]{:S(2)}) %collective-permute-start.3) | collective-permute-done | bytes 8224 | tf_op jit(solution)/shard_map/ppermute | solution.py:32
  10.8 0.0 collective-permute-done.2.near_ref
  (3 shorter events, 0.1 us)
Async XLA Ops:
  0.0 5.0 %collective-permute-start = (bf16[2,2,16,16]{3,2,1,0:T(8,128)(2,1)}, bf16[2,2,16,16]{3,2,1,0:T(8,128)(2,1)S(1)}, u32[]{:S(2)}, u32[]{:S(2)}) collective-permute-start(bf16[2,2,16,16]{3,2,1,0:T(8,128)(2,1)} %refs_7_.1), channel_id=1, source_target_pairs={{1,2},{2,1},{3,0},{0,3},{5,6},{6,5},{7,4},{4,7},{9,10},{10,9},{11,... | collective-permute-start | bytes 6152 | tf_op jit(solution)/shard_map/ppermute | solution.py:22
  2.4 2.7 %collective-permute-start.1 = (bf16[2,2,16,16]{3,2,1,0:T(8,128)(2,1)}, bf16[2,2,16,16]{3,2,1,0:T(8,128)(2,1)S(1)}, u32[]{:S(2)}, u32[]{:S(2)}) collective-permute-start(bf16[2,2,16,16]{3,2,1,0:T(8,128)(2,1)} %refs_7_.1), channel_id=1, source_target_pairs={{0,1},{1,0},{2,3},{3,2},{4,5},{5,4},{6,7},{7,6},{8,9},{9,8},{10,11... | collective-permute-start | bytes 6152 | tf_op jit(solution)/shard_map/ppermute | solution.py:22
  5.2 4.8 %collective-permute-start.4 = (bf16[2,16,128]{2,1,0:T(8,128)(2,1)S(1)}, bf16[2,16,128]{2,1,0:T(8,128)(2,1)S(1)}, u32[]{:S(2)}, u32[]{:S(2)}) collective-permute-start(bf16[2,16,128]{2,1,0:T(8,128)(2,1)S(1)} %shard_map.83.own_ref), channel_id=1, source_target_pairs={{0,4},{1,5},{2,6},{3,7},{4,8},{5,9},{6,10},{7,11},{8,1},{9,0},{10,... | collective-permute-start | bytes 24584 | tf_op jit(solution)/shard_map/ppermute | solution.py:32
  6.8 4.0 %collective-permute-start.3 = (bf16[2,16,128]{2,1,0:T(8,128)(2,1)S(1)}, bf16[2,16,128]{2,1,0:T(8,128)(2,1)S(1)}, u32[]{:S(2)}, u32[]{:S(2)}) collective-permute-start(bf16[2,16,128]{2,1,0:T(8,128)(2,1)S(1)} %shard_map.83.own_ref), channel_id=1, source_target_pairs={{0,8},{1,9},{2,10},{3,11},{4,12},{5,13},{6,14},{7,15},{8,1},{9,0},... | collective-permute-start | bytes 24584 | tf_op jit(solution)/shard_map/ppermute | solution.py:32
  7.9 2.9 %collective-permute-start.2 = (bf16[2,16,128]{2,1,0:T(8,128)(2,1)S(1)}, bf16[2,16,128]{2,1,0:T(8,128)(2,1)S(1)}, u32[]{:S(2)}, u32[]{:S(2)}) collective-permute-start(bf16[2,16,128]{2,1,0:T(8,128)(2,1)S(1)} %shard_map.83.own_ref), channel_id=1, source_target_pairs={{0,1},{1,0},{2,3},{3,2},{4,5},{5,4},{6,7},{7,6},{8,12},{9,13},{10,... | collective-permute-start | bytes 24584 | tf_op jit(solution)/shard_map/ppermute | solution.py:32

commit v7 on v6

--- a/solution.py
+++ b/solution.py
@@ -56,13 +56,9 @@
     even, odd = even_ref[...], odd_ref[...]
     above = jnp.where(space > 0, jnp.where(is_even, odd, even), jnp.zeros_like(even))
     below = jnp.where(space < count - 1, jnp.where(is_even, even, odd), jnp.zeros_like(even))
-    channel = lax.broadcasted_iota(jnp.int32, (width, LANES), 0)
-    lane = lax.broadcasted_iota(jnp.int32, (width, LANES), 1)
-    total = jnp.zeros((frames * cols, LANES), jnp.float32)
-    for r, block in enumerate([x[:, r] for x in (above, own_ref[...], below) for r in range(rows)]):
-        spread = (lane == channel + r * width).astype(own_ref.dtype)
-        total += jnp.dot(block.reshape(frames * cols, width), spread, preferred_element_type=jnp.float32)
-    packed_ref[...] = total.astype(own_ref.dtype).reshape(packed_ref.shape)
+    pieces = [x[:, r].reshape(frames * cols, width) for x in (above, own_ref[...], below) for r in range(rows)]
+    blank = jnp.zeros((frames * cols, LANES - 3 * rows * width), packed_ref.dtype)
+    packed_ref[...] = jnp.concatenate(pieces + [blank], axis=1).reshape(packed_ref.shape)
 
 
 def column_shift(x, by, cols):

time: 11.1 us -> 11 us (level)
  no operation moved by 1% of the time
where the time goes in v7:
time: 11 us; the launch traced here: 10.8 us
  starting transfers between devices  5.87 us (53%)
  Pallas kernels  4.14 us (38%)
  waiting for transfers between devices  0.75 us (7%)
    ppermute x2, starting transfers between devices, swapped(): return lax.ppermute(x, axis, pairs)  3.05 us
    ppermute x3, starting transfers between devices, moved(): return lax.ppermute(x, ('tm', 'space'), pairs)  2.82 us
    pallas_call x1, Pallas kernels, shards(): pl.pallas_call(functools.partial(first_kernel, rows=rows, width=width), o...  1.99 us
    pallas_call x1, Pallas kernels, shards(): pl.pallas_call(stage_kernel, out_shape=[pltpu.VMEM(x.shape, x.dtype) for...  1.98 us
    ppermute x3, waiting for transfers between devices, moved(): return lax.ppermute(x, ('tm', 'space'), pairs)  0.74 us
  transfers between devices with their start and end apart: 5, of which 1 were waited for; matrix products, arithmetic and copies ran while one was open for 0% of the time, Pallas kernels for 37%

profile of v7, /device:TPU:0, one launch (start us, length us, event | category | flops | bytes accessed | tf_op | source)
XLA Modules:
  0.0 10.8 jit_solution(17143134180685871584)
XLA Ops:
  0.0 2.4 %collective-permute-start = (bf16[2,2,16,16]{3,2,1,0:T(8,128)(2,1)}, bf16[2,2,16,16]{3,2,1,0:T(8,128)(2,1)S(1)}, u32[]{:S(2)}, u32[]{:S(2)}) collective-permute-start(bf16[2,2,16,16]{3,2,1,0:T(8,128)(2,1)} %refs_7_.1), channel_id=1, source_target_pairs={{1,2},{2,1},{3,0},{0,3},{5,6},{6,5},{7,4},{4,7},{9,10},{10,9},{11,... | collective-permute-start | bytes 6152 | tf_op jit(solution)/shard_map/ppermute | solution.py:22
  2.4 0.7 %collective-permute-start.1 = (bf16[2,2,16,16]{3,2,1,0:T(8,128)(2,1)}, bf16[2,2,16,16]{3,2,1,0:T(8,128)(2,1)S(1)}, u32[]{:S(2)}, u32[]{:S(2)}) collective-permute-start(bf16[2,2,16,16]{3,2,1,0:T(8,128)(2,1)} %refs_7_.1), channel_id=1, source_target_pairs={{0,1},{1,0},{2,3},{3,2},{4,5},{5,4},{6,7},{7,6},{8,9},{9,8},{10,11... | collective-permute-start | bytes 6152 | tf_op jit(solution)/shard_map/ppermute | solution.py:22
  3.1 2.0 %shard_map.82 = (bf16[1152,768]{1,0:T(8,128)(2,1)S(1)}, bf16[1728,384]{1,0:T(8,128)(2,1)S(1)}, bf16[432,384]{1,0:T(8,128)(2,1)S(1)}, f32[384]{0:T(512)S(1)}, f32...) custom-call(bf16[1152,768]{1,0:T(8,128)(2,1)} %bitcast.6, ...), custom_call_target="tpu_custom_call" | custom-call | tf_op jit(solution)/shard_map/pallas_call | solution.py:235
  5.0 0.0 collective-permute-done.odd_ref
  5.1 0.0 collective-permute-done.1.even_ref
  5.1 0.1 shard_map.83.own_ref
  5.2 1.6 %collective-permute-start.4 = (bf16[2,16,128]{2,1,0:T(8,128)(2,1)S(1)}, bf16[2,16,128]{2,1,0:T(8,128)(2,1)S(1)}, u32[]{:S(2)}, u32[]{:S(2)}) collective-permute-start(bf16[2,16,128]{2,1,0:T(8,128)(2,1)S(1)} %shard_map.83.own_ref), channel_id=1, source_target_pairs={{0,4},{1,5},{2,6},{3,7},{4,8},{5,9},{6,10},{7,11},{8,1},{9,0},{10,... | collective-permute-start | bytes 24584 | tf_op jit(solution)/shard_map/ppermute | solution.py:32
  6.8 1.1 %collective-permute-start.3 = (bf16[2,16,128]{2,1,0:T(8,128)(2,1)S(1)}, bf16[2,16,128]{2,1,0:T(8,128)(2,1)S(1)}, u32[]{:S(2)}, u32[]{:S(2)}) collective-permute-start(bf16[2,16,128]{2,1,0:T(8,128)(2,1)S(1)} %shard_map.83.own_ref), channel_id=1, source_target_pairs={{0,8},{1,9},{2,10},{3,11},{4,12},{5,13},{6,14},{7,15},{8,1},{9,0},... | collective-permute-start | bytes 24584 | tf_op jit(solution)/shard_map/ppermute | solution.py:32
  7.9 0.1 collective-permute-start.2
  8.0 2.0 %shard_map.84 = (bf16[4,2,2,32,192]{4,3,2,1,0:T(8,128)(2,1)}, bf16[2,3,768,192]{3,2,1,0:T(8,128)(2,1)S(1)}) custom-call(bf16[2,16,128]{2,1,0:T(8,128)(2,1)S(1)} %shard_map.83.own_ref, bf16[432,384]{1,0:T(8,128)(2,1)S(1)} %get-tuple-element.16.w_in_ref, f32[384]{0:T(512)S(1)} %get-tuple-element.17.b_in_ref, f32[384]{0:T(512)S(1)} %get-tuple-element.18.gain_ref, ...), custom_call_target="tpu_custom_call" | custom-call | tf_op jit(solution)/shard_map/pallas_call | solution.py:261
  10.0 0.0 collective-permute-done.4.one_ref.near_ref
  10.0 0.7 %collective-permute-done.3.two_ref = bf16[2,16,128]{2,1,0:T(8,128)(2,1)S(1)} collective-permute-done((bf16[2,16,128]{2,1,0:T(8,128)(2,1)S(1)}, bf16[2,16,128]{2,1,0:T(8,128)(2,1)S(1)}, u32[]{:S(2)}, u32[]{:S(2)}) %collective-permute-start.3) | collective-permute-done | bytes 8224 | tf_op jit(solution)/shard_map/ppermute | solution.py:32
  10.8 0.0 collective-permute-done.2.near_ref
  (3 shorter events, 0.1 us)
Async XLA Ops:
  0.0 5.0 %collective-permute-start = (bf16[2,2,16,16]{3,2,1,0:T(8,128)(2,1)}, bf16[2,2,16,16]{3,2,1,0:T(8,128)(2,1)S(1)}, u32[]{:S(2)}, u32[]{:S(2)}) collective-permute-start(bf16[2,2,16,16]{3,2,1,0:T(8,128)(2,1)} %refs_7_.1), channel_id=1, source_target_pairs={{1,2},{2,1},{3,0},{0,3},{5,6},{6,5},{7,4},{4,7},{9,10},{10,9},{11,... | collective-permute-start | bytes 6152 | tf_op jit(solution)/shard_map/ppermute | solution.py:22
  2.4 2.7 %collective-permute-start.1 = (bf16[2,2,16,16]{3,2,1,0:T(8,128)(2,1)}, bf16[2,2,16,16]{3,2,1,0:T(8,128)(2,1)S(1)}, u32[]{:S(2)}, u32[]{:S(2)}) collective-permute-start(bf16[2,2,16,16]{3,2,1,0:T(8,128)(2,1)} %refs_7_.1), channel_id=1, source_target_pairs={{0,1},{1,0},{2,3},{3,2},{4,5},{5,4},{6,7},{7,6},{8,9},{9,8},{10,11... | collective-permute-start | bytes 6152 | tf_op jit(solution)/shard_map/ppermute | solution.py:22
  5.2 4.8 %collective-permute-start.4 = (bf16[2,16,128]{2,1,0:T(8,128)(2,1)S(1)}, bf16[2,16,128]{2,1,0:T(8,128)(2,1)S(1)}, u32[]{:S(2)}, u32[]{:S(2)}) collective-permute-start(bf16[2,16,128]{2,1,0:T(8,128)(2,1)S(1)} %shard_map.83.own_ref), channel_id=1, source_target_pairs={{0,4},{1,5},{2,6},{3,7},{4,8},{5,9},{6,10},{7,11},{8,1},{9,0},{10,... | collective-permute-start | bytes 24584 | tf_op jit(solution)/shard_map/ppermute | solution.py:32
  6.8 4.0 %collective-permute-start.3 = (bf16[2,16,128]{2,1,0:T(8,128)(2,1)S(1)}, bf16[2,16,128]{2,1,0:T(8,128)(2,1)S(1)}, u32[]{:S(2)}, u32[]{:S(2)}) collective-permute-start(bf16[2,16,128]{2,1,0:T(8,128)(2,1)S(1)} %shard_map.83.own_ref), channel_id=1, source_target_pairs={{0,8},{1,9},{2,10},{3,11},{4,12},{5,13},{6,14},{7,15},{8,1},{9,0},... | collective-permute-start | bytes 24584 | tf_op jit(solution)/shard_map/ppermute | solution.py:32
  7.9 2.9 %collective-permute-start.2 = (bf16[2,16,128]{2,1,0:T(8,128)(2,1)S(1)}, bf16[2,16,128]{2,1,0:T(8,128)(2,1)S(1)}, u32[]{:S(2)}, u32[]{:S(2)}) collective-permute-start(bf16[2,16,128]{2,1,0:T(8,128)(2,1)S(1)} %shard_map.83.own_ref), channel_id=1, source_target_pairs={{0,1},{1,0},{2,3},{3,2},{4,5},{5,4},{6,7},{7,6},{8,12},{9,13},{10,... | collective-permute-start | bytes 24584 | tf_op jit(solution)/shard_map/ppermute | solution.py:32

commit v8 on v7

--- a/solution.py
+++ b/solution.py
@@ -125,7 +125,9 @@
     else:
         left = [active[a * block : (a + 2) * block] for a in range(3)]
         w_time = w_time_ref[...]
-    timed = jnp.dot(jnp.concatenate(left, axis=1), w_time, preferred_element_type=jnp.float32)
+    left = jnp.concatenate(left, axis=1)
+    halves = [jnp.dot(left, w_time[:, n : n + features], preferred_element_type=jnp.float32) for n in (0, features)]
+    timed = jnp.concatenate(halves, axis=1)
     upsample(timed + b_time_ref[...][None, :], taps_ref, b_up_ref, out_ref, *scratch, rows, cols)
 
 

time: 11 us -> 11 us (level)
  no operation moved by 1% of the time
where the time goes in v8:
time: 11 us; the launch traced here: 10.8 us
  starting transfers between devices  5.87 us (53%)
  Pallas kernels  4.13 us (38%)
  waiting for transfers between devices  0.76 us (7%)
    ppermute x2, starting transfers between devices, swapped(): return lax.ppermute(x, axis, pairs)  3.05 us
    ppermute x3, starting transfers between devices, moved(): return lax.ppermute(x, ('tm', 'space'), pairs)  2.82 us
    pallas_call x1, Pallas kernels, shards(): pl.pallas_call(stage_kernel, out_shape=[pltpu.VMEM(x.shape, x.dtype) for...  1.98 us
    pallas_call x1, Pallas kernels, shards(): pl.pallas_call(functools.partial(first_kernel, rows=rows, width=width), o...  1.97 us
    ppermute x3, waiting for transfers between devices, moved(): return lax.ppermute(x, ('tm', 'space'), pairs)  0.76 us
  transfers between devices with their start and end apart: 5, of which 1 were waited for; matrix products, arithmetic and copies ran while one was open for 0% of the time, Pallas kernels for 37%

profile of v8, /device:TPU:0, one launch (start us, length us, event | category | flops | bytes accessed | tf_op | source)
XLA Modules:
  0.0 10.8 jit_solution(11560998213144301835)
XLA Ops:
  0.0 2.4 %collective-permute-start = (bf16[2,2,16,16]{3,2,1,0:T(8,128)(2,1)}, bf16[2,2,16,16]{3,2,1,0:T(8,128)(2,1)S(1)}, u32[]{:S(2)}, u32[]{:S(2)}) collective-permute-start(bf16[2,2,16,16]{3,2,1,0:T(8,128)(2,1)} %refs_7_.1), channel_id=1, source_target_pairs={{1,2},{2,1},{3,0},{0,3},{5,6},{6,5},{7,4},{4,7},{9,10},{10,9},{11,... | collective-permute-start | bytes 6152 | tf_op jit(solution)/shard_map/ppermute | solution.py:22
  2.4 0.7 %collective-permute-start.1 = (bf16[2,2,16,16]{3,2,1,0:T(8,128)(2,1)}, bf16[2,2,16,16]{3,2,1,0:T(8,128)(2,1)S(1)}, u32[]{:S(2)}, u32[]{:S(2)}) collective-permute-start(bf16[2,2,16,16]{3,2,1,0:T(8,128)(2,1)} %refs_7_.1), channel_id=1, source_target_pairs={{0,1},{1,0},{2,3},{3,2},{4,5},{5,4},{6,7},{7,6},{8,9},{9,8},{10,11... | collective-permute-start | bytes 6152 | tf_op jit(solution)/shard_map/ppermute | solution.py:22
  3.1 2.0 %shard_map.82 = (bf16[1152,768]{1,0:T(8,128)(2,1)S(1)}, bf16[1728,384]{1,0:T(8,128)(2,1)S(1)}, bf16[432,384]{1,0:T(8,128)(2,1)S(1)}, f32[384]{0:T(512)S(1)}, f32...) custom-call(bf16[1152,768]{1,0:T(8,128)(2,1)} %bitcast.6, ...), custom_call_target="tpu_custom_call" | custom-call | tf_op jit(solution)/shard_map/pallas_call | solution.py:237
  5.0 0.0 collective-permute-done.odd_ref
  5.1 0.0 collective-permute-done.1.even_ref
  5.1 0.1 shard_map.83.own_ref
  5.2 1.6 %collective-permute-start.4 = (bf16[2,16,128]{2,1,0:T(8,128)(2,1)S(1)}, bf16[2,16,128]{2,1,0:T(8,128)(2,1)S(1)}, u32[]{:S(2)}, u32[]{:S(2)}) collective-permute-start(bf16[2,16,128]{2,1,0:T(8,128)(2,1)S(1)} %shard_map.83.own_ref), channel_id=1, source_target_pairs={{0,4},{1,5},{2,6},{3,7},{4,8},{5,9},{6,10},{7,11},{8,1},{9,0},{10,... | collective-permute-start | bytes 24584 | tf_op jit(solution)/shard_map/ppermute | solution.py:32
  6.8 1.1 %collective-permute-start.3 = (bf16[2,16,128]{2,1,0:T(8,128)(2,1)S(1)}, bf16[2,16,128]{2,1,0:T(8,128)(2,1)S(1)}, u32[]{:S(2)}, u32[]{:S(2)}) collective-permute-start(bf16[2,16,128]{2,1,0:T(8,128)(2,1)S(1)} %shard_map.83.own_ref), channel_id=1, source_target_pairs={{0,8},{1,9},{2,10},{3,11},{4,12},{5,13},{6,14},{7,15},{8,1},{9,0},... | collective-permute-start | bytes 24584 | tf_op jit(solution)/shard_map/ppermute | solution.py:32
  7.9 0.1 collective-permute-start.2
  8.0 2.0 %shard_map.84 = (bf16[4,2,2,32,192]{4,3,2,1,0:T(8,128)(2,1)}, bf16[2,3,768,192]{3,2,1,0:T(8,128)(2,1)S(1)}) custom-call(bf16[2,16,128]{2,1,0:T(8,128)(2,1)S(1)} %shard_map.83.own_ref, bf16[432,384]{1,0:T(8,128)(2,1)S(1)} %get-tuple-element.16.w_in_ref, f32[384]{0:T(512)S(1)} %get-tuple-element.17.b_in_ref, f32[384]{0:T(512)S(1)} %get-tuple-element.18.gain_ref, ...), custom_call_target="tpu_custom_call" | custom-call | tf_op jit(solution)/shard_map/pallas_call | solution.py:263
  10.0 0.0 collective-permute-done.4.one_ref.near_ref
  10.0 0.8 %collective-permute-done.3.two_ref = bf16[2,16,128]{2,1,0:T(8,128)(2,1)S(1)} collective-permute-done((bf16[2,16,128]{2,1,0:T(8,128)(2,1)S(1)}, bf16[2,16,128]{2,1,0:T(8,128)(2,1)S(1)}, u32[]{:S(2)}, u32[]{:S(2)}) %collective-permute-start.3) | collective-permute-done | bytes 8224 | tf_op jit(solution)/shard_map/ppermute | solution.py:32
  10.8 0.0 collective-permute-done.2.near_ref
  (3 shorter events, 0.1 us)
Async XLA Ops:
  0.0 5.0 %collective-permute-start = (bf16[2,2,16,16]{3,2,1,0:T(8,128)(2,1)}, bf16[2,2,16,16]{3,2,1,0:T(8,128)(2,1)S(1)}, u32[]{:S(2)}, u32[]{:S(2)}) collective-permute-start(bf16[2,2,16,16]{3,2,1,0:T(8,128)(2,1)} %refs_7_.1), channel_id=1, source_target_pairs={{1,2},{2,1},{3,0},{0,3},{5,6},{6,5},{7,4},{4,7},{9,10},{10,9},{11,... | collective-permute-start | bytes 6152 | tf_op jit(solution)/shard_map/ppermute | solution.py:22
  2.4 2.7 %collective-permute-start.1 = (bf16[2,2,16,16]{3,2,1,0:T(8,128)(2,1)}, bf16[2,2,16,16]{3,2,1,0:T(8,128)(2,1)S(1)}, u32[]{:S(2)}, u32[]{:S(2)}) collective-permute-start(bf16[2,2,16,16]{3,2,1,0:T(8,128)(2,1)} %refs_7_.1), channel_id=1, source_target_pairs={{0,1},{1,0},{2,3},{3,2},{4,5},{5,4},{6,7},{7,6},{8,9},{9,8},{10,11... | collective-permute-start | bytes 6152 | tf_op jit(solution)/shard_map/ppermute | solution.py:22
  5.2 4.8 %collective-permute-start.4 = (bf16[2,16,128]{2,1,0:T(8,128)(2,1)S(1)}, bf16[2,16,128]{2,1,0:T(8,128)(2,1)S(1)}, u32[]{:S(2)}, u32[]{:S(2)}) collective-permute-start(bf16[2,16,128]{2,1,0:T(8,128)(2,1)S(1)} %shard_map.83.own_ref), channel_id=1, source_target_pairs={{0,4},{1,5},{2,6},{3,7},{4,8},{5,9},{6,10},{7,11},{8,1},{9,0},{10,... | collective-permute-start | bytes 24584 | tf_op jit(solution)/shard_map/ppermute | solution.py:32
  6.8 4.0 %collective-permute-start.3 = (bf16[2,16,128]{2,1,0:T(8,128)(2,1)S(1)}, bf16[2,16,128]{2,1,0:T(8,128)(2,1)S(1)}, u32[]{:S(2)}, u32[]{:S(2)}) collective-permute-start(bf16[2,16,128]{2,1,0:T(8,128)(2,1)S(1)} %shard_map.83.own_ref), channel_id=1, source_target_pairs={{0,8},{1,9},{2,10},{3,11},{4,12},{5,13},{6,14},{7,15},{8,1},{9,0},... | collective-permute-start | bytes 24584 | tf_op jit(solution)/shard_map/ppermute | solution.py:32
  7.9 2.9 %collective-permute-start.2 = (bf16[2,16,128]{2,1,0:T(8,128)(2,1)S(1)}, bf16[2,16,128]{2,1,0:T(8,128)(2,1)S(1)}, u32[]{:S(2)}, u32[]{:S(2)}) collective-permute-start(bf16[2,16,128]{2,1,0:T(8,128)(2,1)S(1)} %shard_map.83.own_ref), channel_id=1, source_target_pairs={{0,1},{1,0},{2,3},{3,2},{4,5},{5,4},{6,7},{7,6},{8,12},{9,13},{10,... | collective-permute-start | bytes 24584 | tf_op jit(solution)/shard_map/ppermute | solution.py:32

commit v9 on v8

--- a/solution.py
+++ b/solution.py
@@ -26,9 +26,9 @@
     times, spaces = lax.axis_size("tm"), lax.axis_size("space")
     pairs = []
     for t in range(times):
-        target = target_of(t)
         for s in range(spaces):
-            pairs.append((t * spaces + s, target * spaces + (s ^ 1 if target == t or t - target > 1 else s)))
+            target, tile = target_of(t, s)
+            pairs.append((t * spaces + s, target * spaces + tile))
     return lax.ppermute(x, ("tm", "space"), pairs)
 
 
@@ -250,9 +250,20 @@
         compiler_params=params(1),
     )(odd, even, own)
     times = lax.axis_size("tm")
-    first = moved(own, lambda t: (t + 1) % min(3, times) if t < 3 else t)
-    two = moved(own, lambda t: (t + 2) % times)
-    one = moved(own, lambda t: t if t < 2 else (t - 1) % (times - 2) + 2)
+
+    def in_first(t, s):
+        return (t, s ^ 1) if t > 2 else (0, s ^ 1) if t == 2 else (t + 1, s)
+
+    def by_two(t, s):
+        if t + 2 < times:
+            return t + 2, s
+        last = t == times - 1
+        return (0, s if last else s ^ 1) if s % 2 else (1, s ^ 1 if last else s)
+
+    def in_last(t, s):
+        return (t, s ^ 1) if t < 2 else (2, s) if t == times - 1 else (t + 1, s)
+
+    first, two, one = moved(own, in_first), moved(own, by_two), moved(own, in_last)
 
     scratch = [
         pltpu.VMEM((2, 2, 2 * frames * rows * 2 * cols, LANES), jnp.float32),

time: 11 us -> 11 us (level)
  no operation moved by 1% of the time
where the time goes in v9:
time: 11 us; the launch traced here: 10.8 us
  starting transfers between devices  5.87 us (53%)
  Pallas kernels  4.13 us (38%)
  waiting for transfers between devices  0.76 us (7%)
    ppermute x2, starting transfers between devices, swapped(): return lax.ppermute(x, axis, pairs)  3.05 us
    ppermute x3, starting transfers between devices, moved(): return lax.ppermute(x, ('tm', 'space'), pairs)  2.82 us
    pallas_call x1, Pallas kernels, shards(): pl.pallas_call(stage_kernel, out_shape=[pltpu.VMEM(x.shape, x.dtype) for...  1.98 us
    pallas_call x1, Pallas kernels, shards(): pl.pallas_call(functools.partial(first_kernel, rows=rows, width=width), o...  1.97 us
    ppermute x3, waiting for transfers between devices, moved(): return lax.ppermute(x, ('tm', 'space'), pairs)  0.76 us
  transfers between devices with their start and end apart: 5, of which 1 were waited for; matrix products, arithmetic and copies ran while one was open for 0% of the time, Pallas kernels for 37%

profile of v9, /device:TPU:0, one launch (start us, length us, event | category | flops | bytes accessed | tf_op | source)
XLA Modules:
  0.0 10.8 jit_solution(10357318907831655119)
XLA Ops:
  0.0 2.4 %collective-permute-start = (bf16[2,2,16,16]{3,2,1,0:T(8,128)(2,1)}, bf16[2,2,16,16]{3,2,1,0:T(8,128)(2,1)S(1)}, u32[]{:S(2)}, u32[]{:S(2)}) collective-permute-start(bf16[2,2,16,16]{3,2,1,0:T(8,128)(2,1)} %refs_7_.1), channel_id=1, source_target_pairs={{1,2},{2,1},{3,0},{0,3},{5,6},{6,5},{7,4},{4,7},{9,10},{10,9},{11,... | collective-permute-start | bytes 6152 | tf_op jit(solution)/shard_map/ppermute | solution.py:22
  2.4 0.7 %collective-permute-start.1 = (bf16[2,2,16,16]{3,2,1,0:T(8,128)(2,1)}, bf16[2,2,16,16]{3,2,1,0:T(8,128)(2,1)S(1)}, u32[]{:S(2)}, u32[]{:S(2)}) collective-permute-start(bf16[2,2,16,16]{3,2,1,0:T(8,128)(2,1)} %refs_7_.1), channel_id=1, source_target_pairs={{0,1},{1,0},{2,3},{3,2},{4,5},{5,4},{6,7},{7,6},{8,9},{9,8},{10,11... | collective-permute-start | bytes 6152 | tf_op jit(solution)/shard_map/ppermute | solution.py:22
  3.1 2.0 %shard_map.82 = (bf16[1152,768]{1,0:T(8,128)(2,1)S(1)}, bf16[1728,384]{1,0:T(8,128)(2,1)S(1)}, bf16[432,384]{1,0:T(8,128)(2,1)S(1)}, f32[384]{0:T(512)S(1)}, f32...) custom-call(bf16[1152,768]{1,0:T(8,128)(2,1)} %bitcast.6, ...), custom_call_target="tpu_custom_call" | custom-call | tf_op jit(solution)/shard_map/pallas_call | solution.py:237
  5.0 0.0 collective-permute-done.odd_ref
  5.1 0.0 collective-permute-done.1.even_ref
  5.1 0.1 shard_map.83.own_ref
  5.2 1.6 %collective-permute-start.4 = (bf16[2,16,128]{2,1,0:T(8,128)(2,1)S(1)}, bf16[2,16,128]{2,1,0:T(8,128)(2,1)S(1)}, u32[]{:S(2)}, u32[]{:S(2)}) collective-permute-start(bf16[2,16,128]{2,1,0:T(8,128)(2,1)S(1)} %shard_map.83.own_ref), channel_id=1, source_target_pairs={{0,4},{1,5},{2,6},{3,7},{4,8},{5,9},{6,10},{7,11},{8,1},{9,0},{10,... | collective-permute-start | bytes 24584 | tf_op jit(solution)/shard_map/ppermute | solution.py:32
  6.8 1.1 %collective-permute-start.3 = (bf16[2,16,128]{2,1,0:T(8,128)(2,1)S(1)}, bf16[2,16,128]{2,1,0:T(8,128)(2,1)S(1)}, u32[]{:S(2)}, u32[]{:S(2)}) collective-permute-start(bf16[2,16,128]{2,1,0:T(8,128)(2,1)S(1)} %shard_map.83.own_ref), channel_id=1, source_target_pairs={{0,8},{1,9},{2,10},{3,11},{4,12},{5,13},{6,14},{7,15},{8,4},{9,0},... | collective-permute-start | bytes 24584 | tf_op jit(solution)/shard_map/ppermute | solution.py:32
  7.9 0.1 collective-permute-start.2
  8.0 2.0 %shard_map.84 = (bf16[4,2,2,32,192]{4,3,2,1,0:T(8,128)(2,1)}, bf16[2,3,768,192]{3,2,1,0:T(8,128)(2,1)S(1)}) custom-call(bf16[2,16,128]{2,1,0:T(8,128)(2,1)S(1)} %shard_map.83.own_ref, bf16[432,384]{1,0:T(8,128)(2,1)S(1)} %get-tuple-element.16.w_in_ref, f32[384]{0:T(512)S(1)} %get-tuple-element.17.b_in_ref, f32[384]{0:T(512)S(1)} %get-tuple-element.18.gain_ref, ...), custom_call_target="tpu_custom_call" | custom-call | tf_op jit(solution)/shard_map/pallas_call | solution.py:274
  10.0 0.0 collective-permute-done.4.one_ref.near_ref
  10.0 0.8 %collective-permute-done.3.two_ref = bf16[2,16,128]{2,1,0:T(8,128)(2,1)S(1)} collective-permute-done((bf16[2,16,128]{2,1,0:T(8,128)(2,1)S(1)}, bf16[2,16,128]{2,1,0:T(8,128)(2,1)S(1)}, u32[]{:S(2)}, u32[]{:S(2)}) %collective-permute-start.3) | collective-permute-done | bytes 8224 | tf_op jit(solution)/shard_map/ppermute | solution.py:32
  10.8 0.0 collective-permute-done.2.near_ref
  (3 shorter events, 0.1 us)
Async XLA Ops:
  0.0 5.0 %collective-permute-start = (bf16[2,2,16,16]{3,2,1,0:T(8,128)(2,1)}, bf16[2,2,16,16]{3,2,1,0:T(8,128)(2,1)S(1)}, u32[]{:S(2)}, u32[]{:S(2)}) collective-permute-start(bf16[2,2,16,16]{3,2,1,0:T(8,128)(2,1)} %refs_7_.1), channel_id=1, source_target_pairs={{1,2},{2,1},{3,0},{0,3},{5,6},{6,5},{7,4},{4,7},{9,10},{10,9},{11,... | collective-permute-start | bytes 6152 | tf_op jit(solution)/shard_map/ppermute | solution.py:22
  2.4 2.7 %collective-permute-start.1 = (bf16[2,2,16,16]{3,2,1,0:T(8,128)(2,1)}, bf16[2,2,16,16]{3,2,1,0:T(8,128)(2,1)S(1)}, u32[]{:S(2)}, u32[]{:S(2)}) collective-permute-start(bf16[2,2,16,16]{3,2,1,0:T(8,128)(2,1)} %refs_7_.1), channel_id=1, source_target_pairs={{0,1},{1,0},{2,3},{3,2},{4,5},{5,4},{6,7},{7,6},{8,9},{9,8},{10,11... | collective-permute-start | bytes 6152 | tf_op jit(solution)/shard_map/ppermute | solution.py:22
  5.2 4.8 %collective-permute-start.4 = (bf16[2,16,128]{2,1,0:T(8,128)(2,1)S(1)}, bf16[2,16,128]{2,1,0:T(8,128)(2,1)S(1)}, u32[]{:S(2)}, u32[]{:S(2)}) collective-permute-start(bf16[2,16,128]{2,1,0:T(8,128)(2,1)S(1)} %shard_map.83.own_ref), channel_id=1, source_target_pairs={{0,4},{1,5},{2,6},{3,7},{4,8},{5,9},{6,10},{7,11},{8,1},{9,0},{10,... | collective-permute-start | bytes 24584 | tf_op jit(solution)/shard_map/ppermute | solution.py:32
  6.8 4.0 %collective-permute-start.3 = (bf16[2,16,128]{2,1,0:T(8,128)(2,1)S(1)}, bf16[2,16,128]{2,1,0:T(8,128)(2,1)S(1)}, u32[]{:S(2)}, u32[]{:S(2)}) collective-permute-start(bf16[2,16,128]{2,1,0:T(8,128)(2,1)S(1)} %shard_map.83.own_ref), channel_id=1, source_target_pairs={{0,8},{1,9},{2,10},{3,11},{4,12},{5,13},{6,14},{7,15},{8,4},{9,0},... | collective-permute-start | bytes 24584 | tf_op jit(solution)/shard_map/ppermute | solution.py:32
  7.9 2.9 %collective-permute-start.2 = (bf16[2,16,128]{2,1,0:T(8,128)(2,1)S(1)}, bf16[2,16,128]{2,1,0:T(8,128)(2,1)S(1)}, u32[]{:S(2)}, u32[]{:S(2)}) collective-permute-start(bf16[2,16,128]{2,1,0:T(8,128)(2,1)S(1)} %shard_map.83.own_ref), channel_id=1, source_target_pairs={{0,1},{1,0},{2,3},{3,2},{4,5},{5,4},{6,7},{7,6},{8,12},{9,13},{10,... | collective-permute-start | bytes 24584 | tf_op jit(solution)/shard_map/ppermute | solution.py:32
